TPU v7x, 512 devices: a whole 4x8x8 slice. The times are simulated.
512 devices in a mesh: seq: 128 (over y, z, core), win: 4 (over x).
Axes of the slice: x: 4, y: 8, z: 8, core: 2. Of those that a mesh axis runs over, the one named last changes fastest.
Arguments:
- queries: bfloat16 [65536, 1024], P(('win', 'seq')), parts along dimension 0, may hold values from -6 to 6
- key_rows: bfloat16 [65536, 1024], P(('win', 'seq')), parts along dimension 0, may hold values from -6 to 6
- value_rows: bfloat16 [65536, 2048], P(('win', 'seq')), parts along dimension 0, may hold values from -6 to 6
- residual: bfloat16 [65536, 1024], P(('win', 'seq')), parts along dimension 0, may hold values from -6 to 6
- out_weight: bfloat16 [2048, 1024], P(None, 'seq'), may hold values from -0.125 to 0.125
- expert_in: bfloat16 [128, 1024, 768], P('seq'), may hold values from -0.1875 to 0.1875
- expert_out: bfloat16 [128, 384, 1024], P('seq'), may hold values from -0.3125 to 0.3125
- expert_ids: int32 [65536, 2], P(('win', 'seq')), parts along dimension 0, may hold values from 0 to 127, all different within a row; in each aligned block of 128 rows (0 to 127, 128 to 255, ...) at most 4 rows name the same one
- gate_values: float32 [65536, 2], P(('win', 'seq')), parts along dimension 0, may hold values from 0.2 to 1
Outputs:
- layer_out: bfloat16 [65536, 1024], P(('win', 'seq')), parts along dimension 0
There are 4 independent parts, one for each index of `win`. A program takes and returns all parts, laid end to end along the dimension named above; an argument that names none is the same for every part. Nothing has to cross between parts.
Inputs may be any that keep to these rules, and one draw needn't show every extreme that they name: `expert_ids`: the 2 ids of a row differ. Within the rows of one block of 128 tokens no expert is named by more than 4 rows, a bound that some block reaches. Every expert is named somewhere.
All inputs are finite; a program needn't handle non-finite values.
Results may differ from a plain program's by a relative error of at most 0.013.
Values may be sent and summed in bfloat16 or wider, within the bound.
A program may use at most 128 MiB of HBM per device.

v0:
```python
import jax
import jax.numpy as jnp
from jax import lax
from jax.sharding import PartitionSpec as P

D = 1024
H = 16
DK = 64
DV = 128
HE = 384
TOP = 2


def carried_in(x, axis, join, neutral):
    place = lax.axis_index(axis)
    gathered = lax.all_gather(x.astype(jnp.bfloat16), axis)
    state = jnp.zeros_like(x) + jnp.asarray(neutral, x.dtype)

    def one(step, state):
        return join(state, lax.dynamic_index_in_dim(gathered, step, 0, False).astype(x.dtype))

    return lax.fori_loop(0, place, one, state)


def add_states(earlier, later):
    return earlier + later


def per_device(
    queries,
    key_rows,
    value_rows,
    residual,
    out_weight,
    expert_in,
    expert_out,
    expert_ids,
    gate_values,
):
    length = queries.shape[0]
    q_heads = queries.reshape(length, H, DK)
    k_heads = key_rows.reshape(length, H, DK)
    v_heads = value_rows.reshape(length, H, DV)
    local_state = jnp.einsum("thd,the->hde", k_heads, v_heads, preferred_element_type=jnp.float32)
    prefix = carried_in(local_state, "seq", add_states, jnp.zeros_like(local_state))
    causal = jnp.arange(length)[:, None] >= jnp.arange(length)[None, :]
    scores = jnp.einsum("thd,shd->hts", q_heads, k_heads, preferred_element_type=jnp.float32)
    scores = jnp.where(causal[None], scores, 0.0).astype(jnp.bfloat16)
    intra_sum = jnp.einsum("hts,she->the", scores, v_heads, preferred_element_type=jnp.float32)
    inter_sum = jnp.einsum(
        "thd,hde->the", q_heads.astype(jnp.float32), prefix, precision=lax.Precision.HIGHEST
    )
    position = (lax.axis_index("seq") * length + jnp.arange(length)).astype(jnp.float32)
    scaling = lax.rsqrt((position + 1.0) * DK)
    attended = (
        ((intra_sum + inter_sum) * scaling[:, None, None])
        .astype(jnp.bfloat16)
        .reshape(length, H * DV)
    )
    projected = jnp.dot(
        attended,
        lax.all_gather(out_weight, "seq", axis=1, tiled=True),
        preferred_element_type=jnp.float32,
    )
    hidden = (residual.astype(jnp.float32) + projected).astype(jnp.bfloat16)
    hidden_float = hidden.astype(jnp.float32)
    normed = (
        hidden_float
        * lax.rsqrt(jnp.mean(hidden_float * hidden_float, axis=-1, keepdims=True) + 1e-06)
    ).astype(jnp.bfloat16)
    experts = lax.axis_size("seq") * expert_in.shape[0]
    capacity = max(2, 2 * length * TOP // experts)
    flat_ids = expert_ids.reshape(-1)
    one_hot = (flat_ids[:, None] == jnp.arange(experts)[None, :]).astype(jnp.int32)
    earlier = jnp.cumsum(one_hot, axis=0) - one_hot
    slot_index = jnp.sum(earlier * one_hot, axis=-1)
    dest_row = flat_ids * capacity + slot_index
    buffer = (
        jnp.zeros((experts * capacity, D), jnp.bfloat16)
        .at[dest_row]
        .set(jnp.repeat(normed, TOP, axis=0))
    )
    buffer = buffer.reshape(experts, 1, capacity, D)
    act = jnp.einsum(
        "ensd,edf->ensf",
        lax.all_to_all(buffer, "seq", split_axis=0, concat_axis=1, tiled=True),
        expert_in,
        preferred_element_type=jnp.float32,
    )
    inner = (jax.nn.silu(act[..., :HE]) * act[..., HE:]).astype(jnp.bfloat16)
    produced_all = jnp.einsum(
        "ensf,efd->ensd", inner, expert_out, preferred_element_type=jnp.float32
    ).astype(jnp.bfloat16)
    returned_rows = lax.all_to_all(produced_all, "seq", split_axis=1, concat_axis=0, tiled=True)
    picked = returned_rows.reshape(experts * capacity, D)[dest_row]
    combined = jnp.sum(
        picked.astype(jnp.float32).reshape(length, TOP, D) * gate_values[:, :, None], axis=1
    )
    return (hidden_float + combined).astype(jnp.bfloat16)


def solution(mesh):
    in_specs = (
        P(("win", "seq"), None),
        P(("win", "seq"), None),
        P(("win", "seq"), None),
        P(("win", "seq"), None),
        P(None, "seq"),
        P("seq", None, None),
        P("seq", None, None),
        P(("win", "seq"), None),
        P(("win", "seq"), None),
    )
    out_specs = P(("win", "seq"), None)
    return jax.shard_map(
        per_device, mesh=mesh, in_specs=in_specs, out_specs=out_specs, check_vma=False
    )
```

profile of v0, /device:TPU:1, one launch (start us, length us, event | category | flops | bytes accessed | tf_op | source)
XLA Modules:
  0.0 401.6 jit_solution(2190676096343332066)
XLA Ops:
  6.5 0.0 copy-start
  6.5 0.0 copy-start.2
  6.5 0.0 copy-start.1
  6.5 0.0 all-gather.6.cloned.1.call-start
  6.5 1.2 copy.28
  7.8 2.0 convolution_convert_fusion.1
  9.8 0.0 all-gather.6.cloned.1.call-update
  9.9 0.0 all-gather.4.cloned.1.call-start
  9.9 0.7 all-gather.4.cloned.1.call-update
  10.6 0.0 copy-done.2
  10.6 0.1 copy.32
  10.7 0.1 eq.29
  10.9 0.1 eq.25
  11.0 0.0 copy-done.1
  11.0 0.2 copy.27
  11.2 0.1 copy.34
  11.3 0.2 fusion.26
  11.6 0.1 copy.31
  11.7 0.1 mul.73
  11.9 0.2 fusion.28
  12.1 1.7 convolution_bitcast_fusion.1
  13.9 144.1 %all-gather.6.cloned.1.call-done = bf16[2048,64,128]{2,1,0:T(8,128)(2,1)} async-done(((bf16[16,64,128]{2,1,0:T(8,128)(2,1)}), bf16[2048,64,128]{2,1,0:T(8,128)(2,1)}) %all-gather.6.cloned.1.call-update) | async-done | bytes 33554448 | tf_op jit(solution)/shard_map/all_gather | solution.py:16
  158.0 1.1 while.10
  158.0 1.1 convert_add_fusion.2
  159.1 1.8 fusion.8
  160.9 82.8 %all-gather.4.cloned.1.call-done = bf16[2048,1024]{0,1:T(8,128)(2,1)} async-done(((bf16[2048,8]{0,1:T(8,128)(2,1)}), bf16[2048,1024]{0,1:T(8,128)(2,1)}) %all-gather.4.cloned.1.call-update) | async-done | bytes 4194320 | tf_op jit(solution)/shard_map/all_gather | solution.py:62
  243.7 4.0 multiply_reduce_fusion.1
  247.7 0.1 multiply_convert_fusion
  247.8 0.3 broadcast_in_dim.34
  248.1 1.0 reshape.151
  249.1 2.4 scatter_custom_fusion
  251.5 1.2 reshape.131
  252.7 93.0 %all_to_all.8 = bf16[128,1,4,1024]{3,2,1,0:T(4,128)(2,1)S(1)} all-to-all(bf16[128,1,4,1024]{3,2,1,0:T(4,128)(2,1)} %bitcast.76), channel_id=1, replica_groups=mesh['seq'=128,'win'=4] {'seq'}, dimensions={0} | all-to-all | bytes 2097152 | tf_op jit(solution)/shard_map/all_to_all | solution.py:86
  345.7 0.0 copy-done
  345.7 0.0 copy-start.4
  345.7 1.4 fusion.2
  347.1 0.0 copy-done.4
  347.1 0.7 fusion.5
  347.8 1.8 copy.38
  349.7 7.9 %all-to-all-start.1 = ((bf16[1,128,4,1024]{3,2,0,1:T(4,128)(2,1)}), bf16[1,128,4,1024]{3,2,0,1:T(4,128)(2,1)}, u32[]{:S(2)}, u32[]{:S(2)}) async-start(bf16[1,128,4,1024]{3,2,0,1:T(4,128)(2,1)} %copy.38), calls=%async_computation.1 | async-start | bytes 2097152 | tf_op jit(solution)/shard_map/all_to_all | solution.py:94
  357.6 0.0 copy-done.3
  357.6 0.1 copy.39
  357.7 29.9 %all-to-all-done.1 = bf16[1,128,4,1024]{3,2,0,1:T(4,128)(2,1)} async-done(((bf16[1,128,4,1024]{3,2,0,1:T(4,128)(2,1)}), bf16[1,128,4,1024]{3,2,0,1:T(4,128)(2,1)}, u32[]{:S(2)}, u32[]{:S(2)}) %all-to-all-start.1) | async-done | bytes 1048608 | tf_op jit(solution)/shard_map/all_to_all | solution.py:94
  387.6 1.3 reshape.136
  389.0 2.0 gather_fusion
  390.9 1.7 reshape.138
  392.6 1.3 multiply_reduce_fusion
  394.0 0.8 add_convert_fusion
  (14 shorter events, 0.2 us)
Async XLA Ops:
  6.5 339.2 %copy-start = (bf16[1,1024,768]{2,1,0:T(8,128)(2,1)S(1)}, bf16[1,1024,768]{2,1,0:T(8,128)(2,1)}, u32[]{:S(2)}) copy-start(bf16[1,1024,768]{2,1,0:T(8,128)(2,1)} %param.16) | copy-start | bytes 4718596
  6.5 4.1 %copy-start.2 = (s32[128,2]{0,1:T(2,128)S(1)}, s32[128,2]{0,1:T(2,128)}, u32[]{:S(2)}) copy-start(s32[128,2]{0,1:T(2,128)} %param.18) | copy-start | bytes 3076
  6.5 4.5 %copy-start.1 = (bf16[128,1024]{1,0:T(8,128)(2,1)S(1)}, bf16[128,1024]{1,0:T(8,128)(2,1)}, u32[]{:S(2)}) copy-start(bf16[128,1024]{1,0:T(8,128)(2,1)} %param.11) | copy-start | bytes 786436
  6.5 151.4 %all-gather.6.cloned.1.call-start = ((), (), s32[]{:S(2)}) async-start(), calls=%async_computation.3 | async-start | bytes 33816576 | tf_op jit(solution)/shard_map/all_gather | solution.py:16
  9.9 233.9 %all-gather.4.cloned.1.call-start = ((), (), s32[]{:S(2)}) async-start(), calls=%async_computation.2 | async-start | bytes 4227072 | tf_op jit(solution)/shard_map/all_gather | solution.py:62
  345.7 1.4 copy-start.4
  349.7 7.9 %copy-start.3 = (f32[128,2]{0,1:T(2,128)S(1)}, f32[128,2]{0,1:T(2,128)}, u32[]{:S(2)}) copy-start(f32[128,2]{0,1:T(2,128)} %param.19) | copy-start | bytes 3076
  349.7 37.9 %all-to-all-start.1 = ((bf16[1,128,4,1024]{3,2,0,1:T(4,128)(2,1)}), bf16[1,128,4,1024]{3,2,0,1:T(4,128)(2,1)}, u32[]{:S(2)}, u32[]{:S(2)}) async-start(bf16[1,128,4,1024]{3,2,0,1:T(4,128)(2,1)} %copy.38), calls=%async_computation.1 | async-start | bytes 2097152 | tf_op jit(solution)/shard_map/all_to_all | solution.py:94
Sparse Core Ops, SparseCore 0:
  10.5 147.4 all-gather.5
  161.1 82.5 all-gather.3
where the time goes:
time: 406 us; the launch traced here: 402 us
  waiting for transfers between devices  257 us (63%)
  blocking collectives  93 us (23%)
  local copies, waits for them, and re-layouts  14.1 us (3%)
  between operations  13.6 us (3%)
  matrix products  11.6 us (3%)
  starting transfers between devices  7.94 us (2%)
    all_gather x1, waiting for transfers between devices, carried_in(): gathered = lax.all_gather(x.astype(jnp.bfloat16), axis)  144 us
    all_to_all x1, blocking collectives, per_device(): lax.all_to_all(buffer, 'seq', split_axis=0, concat_axis=1, tiled=True)  93 us
    all_gather x1, waiting for transfers between devices, per_device(): lax.all_gather(out_weight, 'seq', axis=1, tiled=True)  82.8 us
    all_to_all x1, waiting for transfers between devices, per_device(): lax.all_to_all(produced_all, 'seq', split_axis=1, concat_axis=0, tiled=True)  29.9 us
  transfers between devices with their start and end apart: 3, of which 3 were waited for; matrix products, arithmetic and copies ran while one was open for 2% of the time, Pallas kernels for 0%

commit v1 on v0

v1 whole, which is shorter than its diff:
```python
import functools

import jax
import jax.numpy as jnp
from jax import lax
from jax.experimental import pallas as pl
from jax.experimental.pallas import tpu as pltpu
from jax.sharding import PartitionSpec as P

TOP = 2
CAP = 4
GROUPS = 4
MESH = pl.DeviceIdType.MESH
BF = jnp.bfloat16
F32 = jnp.float32


def dot(a, b, dims=((1,), (0,))):
    return lax.dot_general(a, b, (dims, ((), ())), preferred_element_type=F32)


def layer_kernel(
    ny,
    nz,
    heads,
    dk,
    dv,
    q_ref,
    k_ref,
    v_ref,
    res_ref,
    wt_ref,
    win_hbm,
    wout_hbm,
    ids_ref,
    gates_ref,
    o_ref,
    s_loc,
    tot,
    p_out,
    r1,
    r2,
    r3,
    w_loc,
    w_all,
    intra,
    attended,
    win,
    wout,
    xb,
    xr,
    yb,
    ret,
    s1_send,
    s1_recv,
    s2_send,
    s2_recv,
    s3_send,
    s3_recv,
    w1_send,
    w1_recv,
    ring_send,
    ring_recv,
    sib_send,
    sib_recv,
    x_send,
    x_recv,
    y_send,
    y_recv,
    win_sem,
):
    n = ny * nz * 2
    row = nz * 2
    length = q_ref.shape[0]
    width = res_ref.shape[1]
    he = wout.shape[0]
    quarter = w_loc.shape[2]
    me = lax.axis_index("seq")
    y, z, c = me // row, lax.rem(me // 2, nz), lax.rem(me, 2)
    at_row = lax.rem(me, row)

    def seq(yy, zz, cc):
        return yy * row + zz * 2 + cc

    def remote(src, dst, ssem, rsem, dev):
        return pltpu.make_async_remote_copy(
            src_ref=src,
            dst_ref=dst,
            send_sem=ssem,
            recv_sem=rsem,
            device_id={"seq": dev},
            device_id_type=MESH,
        )

    def drain(ref, sem):
        pltpu.make_async_copy(ref, ref, sem).wait()

    barrier = pltpu.get_barrier_semaphore()

    def greet(i, _):
        pl.semaphore_signal(
            barrier, inc=1, device_id={"seq": lax.rem(me + i, n)}, device_id_type=MESH
        )
        return 0

    lax.fori_loop(1, n, greet, 0)

    load_in = pltpu.make_async_copy(win_hbm, win, win_sem.at[0])
    load_out = pltpu.make_async_copy(wout_hbm, wout, win_sem.at[1])
    load_in.start()
    load_out.start()

    def states(p, _):
        kp = k_ref[:, pl.ds(pl.multiple_of(p * 2 * dk, 2 * dk), 2 * dk)]
        vp = v_ref[:, pl.ds(pl.multiple_of(p * 2 * dv, 2 * dv), 2 * dv)]
        kv = dot(kp, vp, ((0,), (0,)))
        s_loc[2 * p] = kv[:dk, :dv].astype(BF)
        s_loc[2 * p + 1] = kv[dk:, dv:].astype(BF)
        return 0

    lax.fori_loop(0, heads // 2, states, 0)
    for part in range(4):
        w_loc[part] = wt_ref[:, part * quarter : (part + 1) * quarter]

    pl.semaphore_wait(barrier, n - 1)

    pltpu.make_async_copy(s_loc.at[at_row], r1.at[at_row], s1_recv).start()

    def phase1(i, _):
        to = lax.rem(at_row + i, row)
        remote(s_loc.at[to], r1.at[at_row], s1_send, s1_recv, y * row + to).start()
        return 0

    lax.fori_loop(1, row, phase1, 0)

    def own_part(part, which):
        pltpu.make_async_copy(
            w_loc.at[part], w_all.at[part, y, z, c], w1_recv.at[which]
        ).start()

    own_part(2 * c, 0)
    own_part(2 * c + 1, 1)

    def along_z(i, _):
        to = lax.rem(at_row + i, row)
        part = 2 * lax.rem(to, 2)
        remote(
            w_loc.at[part], w_all.at[part, y, z, c], w1_send, w1_recv.at[0], y * row + to
        ).start()
        return 0

    def along_y(i, _):
        cc = lax.rem(c + i, 2)
        yy = lax.rem(y + i // 2, ny)
        part = 2 * cc + 1
        remote(
            w_loc.at[part], w_all.at[part, y, z, c], w1_send, w1_recv.at[1], seq(yy, z, cc)
        ).start()
        return 0

    lax.fori_loop(1, row, along_z, 0)
    lax.fori_loop(1, 2 * ny, along_y, 0)

    t_row = lax.broadcasted_iota(jnp.int32, (2 * length, length), 0)
    t_col = lax.broadcasted_iota(jnp.int32, (2 * length, length), 1)
    causal = lax.rem(t_row, length) >= t_col
    first = lax.broadcasted_iota(jnp.int32, (length, 2 * dk), 1) < dk

    def two_heads(p):
        qp = q_ref[:, pl.ds(pl.multiple_of(p * 2 * dk, 2 * dk), 2 * dk)]
        zero = jnp.zeros_like(qp)
        return jnp.concatenate(
            [jnp.where(first, qp, zero), jnp.where(first, zero, qp)], axis=0
        )

    def inside(p, _):
        kp = k_ref[:, pl.ds(pl.multiple_of(p * 2 * dk, 2 * dk), 2 * dk)]
        at = pl.multiple_of(p * 2 * dv, 2 * dv)
        scores = dot(two_heads(p), kp, ((1,), (1,)))
        scores = jnp.where(causal, scores, 0.0).astype(BF)
        vp = v_ref[:, pl.ds(at, 2 * dv)]
        intra[:, pl.ds(at, dv)] = dot(scores[:length], vp[:, :dv])
        intra[:, pl.ds(pl.multiple_of(at + dv, dv), dv)] = dot(scores[length:], vp[:, dv:])
        return 0

    half = heads // 4
    lax.fori_loop(0, half, inside, 0)

    drain(r1, s1_recv)
    total = r1[0].astype(F32)
    for i in range(1, row):
        total = total + r1[i].astype(F32)
    tot[...] = total.astype(BF)
    pltpu.make_async_copy(tot, r2.at[y], s2_recv).start()

    def phase2(i, _):
        yy = lax.rem(y + i, ny)
        remote(tot, r2.at[y], s2_send, s2_recv, seq(yy, z, c)).start()
        return 0

    lax.fori_loop(1, ny, phase2, 0)

    pa, pb = 2 * c, 2 * c + 1
    sib = seq(y, z, 1 - c)

    def a_block(yy):
        return w_all.at[pa, yy]

    def b_block(zz):
        return w_all.at[pb, :, zz]

    def a_half(yy, h):
        return w_all.at[pa, yy, pl.ds(h * (nz // 2), nz // 2)]

    def b_half(zz, h):
        return w_all.at[pb, pl.ds(h * (ny // 2), ny // 2), zz]

    def mod_y(v):
        return lax.rem(v + 2 * ny, ny)

    def mod_z(v):
        return lax.rem(v + 2 * nz, nz)

    def to_sibling(block):
        remote(block, block, sib_send, sib_recv, sib).start()

    ring = []

    def ring_copy(axis, way, step):
        size, mod, at = (ny, mod_y, y) if axis == 0 else (nz, mod_z, z)
        block, part = (a_block, a_half) if axis == 0 else (b_block, b_half)
        sign = 1 if way == 0 else -1
        origin = mod(at - sign * (step - 1))
        target = mod(at + sign)
        dev = seq(target, z, c) if axis == 0 else seq(y, target, c)
        ref = part(origin, way) if 2 * step == size else block(origin)
        return remote(
            ref, ref, ring_send.at[axis, way, step - 1], ring_recv.at[axis, way, step - 1], dev
        )

    def ring_got(axis, way, step):
        size, mod, at = (ny, mod_y, y) if axis == 0 else (nz, mod_z, z)
        block, part = (a_block, a_half) if axis == 0 else (b_block, b_half)
        origin = mod(at - step if way == 0 else at + step)
        ref = part(origin, way) if 2 * step == size else block(origin)
        drain(ref, ring_recv.at[axis, way, step - 1])
        return ref

    def ring_step(axis, step):
        size = ny if axis == 0 else nz
        if step > size // 2:
            return
        for way in (0, 1):
            got = ring_got(axis, way, step)
            if 2 * (step + 1) <= size:
                ring_copy(axis, way, step + 1).start()
            to_sibling(got)

    drain(w_all.at[pa, y], w1_recv.at[0])
    for way in (0, 1):
        ring_copy(0, way, 1).start()
    drain(w_all.at[pb, :, z], w1_recv.at[1])
    for way in (0, 1):
        ring_copy(1, way, 1).start()
    to_sibling(a_block(y))
    to_sibling(b_block(z))

    lax.fori_loop(half, heads // 2, inside, 0)

    drain(r2, s2_recv)
    run = jnp.zeros(total.shape, F32)
    for yy in range(ny):
        run = run + jnp.where(yy < y, r2[yy].astype(F32), 0.0)
    for i in range(row):
        p_out[i] = run.astype(BF)
        if i < row - 1:
            run = run + r1[i].astype(F32)
    pltpu.make_async_copy(p_out.at[at_row], r3.at[at_row], s3_recv).start()

    def phase3(i, _):
        to = lax.rem(at_row + i, row)
        remote(p_out.at[to], r3.at[at_row], s3_send, s3_recv, y * row + to).start()
        return 0

    lax.fori_loop(1, row, phase3, 0)

    for axis in (0, 1):
        ring_step(axis, 1)

    eye = lax.broadcasted_iota(jnp.int32, (length, length), 0) == lax.broadcasted_iota(
        jnp.int32, (length, length), 1
    )
    below = lax.broadcasted_iota(jnp.int32, (length, length), 1) < lax.broadcasted_iota(
        jnp.int32, (length, length), 0
    )
    above = lax.broadcasted_iota(jnp.int32, (length, length), 0) < lax.broadcasted_iota(
        jnp.int32, (length, length), 1
    )

    def column(r):
        return jnp.sum(jnp.where(eye, r, 0.0), axis=1, keepdims=True)

    id_row = [ids_ref[j : j + 1, :].astype(F32) for j in range(TOP)]
    id_col = [column(r) for r in id_row]
    gate_col = [column(gates_ref[j : j + 1, :]) for j in range(TOP)]
    place_row, place_col = [], []
    for j in range(TOP):
        row_count, col_count = 0.0, 0.0
        for i in range(TOP):
            row_count = row_count + jnp.where(above & (id_col[i] == id_row[j]), 1.0, 0.0)
            col_count = col_count + jnp.where(below & (id_col[j] == id_row[i]), 1.0, 0.0)
        place_row.append(id_row[j] * CAP + jnp.sum(row_count, axis=0, keepdims=True))
        place_col.append(id_col[j] * CAP + jnp.sum(col_count, axis=1, keepdims=True))
    rows = n * CAP
    r_iota = lax.broadcasted_iota(jnp.int32, (rows, length), 0).astype(F32)
    spread = jnp.where(
        (r_iota == place_row[0]) | (r_iota == place_row[1]), 1.0, 0.0
    ).astype(BF)

    for axis in (0, 1):
        ring_step(axis, 2)

    drain(r3, s3_recv)
    position = me * length + lax.broadcasted_iota(jnp.int32, (length, 1), 0)
    scaling = lax.rsqrt((position.astype(F32) + 1.0) * dk)
    for p in range(heads // 2):
        earlier = dot(two_heads(p), r3[2 * p : 2 * p + 2].reshape(2 * dk, dv))
        for h in range(2):
            cols = slice((2 * p + h) * dv, (2 * p + h + 1) * dv)
            attended[:, cols] = (
                (intra[:, cols] + earlier[h * length : (h + 1) * length]) * scaling
            ).astype(BF)

    for step in range(3, max(ny, nz) // 2 + 1):
        for axis in (0, 1):
            ring_step(axis, step)
    drain(w_all.at[pl.ds(2 * (1 - c), 2)], sib_recv)

    projected = jnp.zeros((length, width), F32)
    for part in range(4):
        projected = projected + dot(
            attended[:, part * quarter : (part + 1) * quarter],
            w_all[part].reshape(width, quarter),
            ((1,), (1,)),
        )
    hidden = (res_ref[...].astype(F32) + projected).astype(BF)
    hidden_float = hidden.astype(F32)
    intra[:, :width] = hidden_float
    normed = (
        hidden_float
        * lax.rsqrt(jnp.mean(hidden_float * hidden_float, axis=-1, keepdims=True) + 1e-06)
    ).astype(BF)
    xb[...] = dot(spread, normed).astype(BF).reshape(n, CAP, width)

    def offset(i):
        j = lax.rem(i * 37, n)
        return j // row, lax.rem(j // 2, nz), lax.rem(j, 2)

    def ahead(i):
        dy, dz, dc = offset(i)
        return seq(lax.rem(y + dy, ny), lax.rem(z + dz, nz), lax.rem(c + dc, 2))

    def behind(i):
        dy, dz, dc = offset(i)
        return seq(lax.rem(y - dy + ny, ny), lax.rem(z - dz + nz, nz), lax.rem(c - dc + 2, 2))

    per = n // GROUPS
    pltpu.make_async_copy(xb.at[me], xr.at[0], x_recv.at[0]).start()

    def dispatch(i, _):
        to = ahead(i)
        remote(xb.at[to], xr.at[i], x_send, x_recv.at[i // per], to).start()
        return 0

    lax.fori_loop(1, n, dispatch, 0)

    load_in.wait()
    load_out.wait()

    def expert(g):
        lo = g * per
        drain(xr.at[pl.ds(lo, per)], x_recv.at[g])
        x = xr[pl.ds(lo, per)].reshape(per * CAP, width)
        act = dot(x, win[...])
        gate, up = act[:, :he], act[:, he:]
        inner = (gate / (1.0 + jnp.exp(-gate)) * up).astype(BF)
        yb[pl.ds(lo, per)] = dot(inner, wout[...]).astype(BF).reshape(per, CAP, width)

    def give_back(i, _):
        to = behind(i)
        remote(yb.at[i], ret.at[me], y_send, y_recv, to).start()
        return 0

    expert(0)
    pltpu.make_async_copy(yb.at[0], ret.at[me], y_recv).start()
    lax.fori_loop(1, per, give_back, 0)

    def group(g, _):
        expert(g)
        lax.fori_loop(g * per, (g + 1) * per, give_back, 0)
        return 0

    lax.fori_loop(1, GROUPS, group, 0)

    r_lane = lax.broadcasted_iota(jnp.int32, (length, rows), 1).astype(F32)
    picks = [jnp.where(r_lane == place_col[j], 1.0, 0.0).astype(BF) for j in range(TOP)]
    drain(ret, y_recv)
    back = ret[...].reshape(rows, width)
    combined = dot(picks[0], back) * gate_col[0] + dot(picks[1], back) * gate_col[1]
    o_ref[...] = (intra[:, :width] + combined).astype(BF)

    drain(s_loc.at[pl.ds(0, row - 1)], s1_send)
    drain(r2.at[pl.ds(0, ny - 1)], s2_send)
    drain(p_out.at[pl.ds(0, row - 1)], s3_send)
    for _ in range(2):
        drain(w_loc.at[0], w1_send)
    for _ in range(row - 2 + 2 * ny - 2):
        drain(w_loc.at[0], w1_send)
    for axis, size in ((0, ny), (1, nz)):
        for step in range(1, size // 2 + 1):
            for way in (0, 1):
                ring_copy(axis, way, step).wait_send()
    drain(w_all.at[pl.ds(2 * c, 2)], sib_send)
    drain(xb.at[pl.ds(0, n - 1)], x_send)
    drain(yb.at[pl.ds(0, n - 1)], y_send)


def layer(ny, nz, heads, dk, dv, q, k, v, res, wt, w_in, w_out, ids, gates):
    n = ny * nz * 2
    row = nz * 2
    length, width = res.shape
    cols = wt.shape[0]
    quarter = heads * dv // 4
    vmem = pl.BlockSpec(memory_space=pltpu.VMEM)
    hbm = pl.BlockSpec(memory_space=pl.ANY)
    steps = max(ny, nz) // 2
    dma = pltpu.SemaphoreType.DMA
    rows = (n, CAP, width)
    return pl.pallas_call(
        functools.partial(layer_kernel, ny, nz, heads, dk, dv),
        out_shape=jax.ShapeDtypeStruct((length, width), BF),
        in_specs=[vmem] * 5 + [hbm] * 2 + [vmem] * 2,
        out_specs=vmem,
        scratch_shapes=[
            pltpu.VMEM((heads, dk, dv), BF),
            pltpu.VMEM((dk, dv), BF),
            pltpu.VMEM((row, dk, dv), BF),
            pltpu.VMEM((row, dk, dv), BF),
            pltpu.VMEM((ny, dk, dv), BF),
            pltpu.VMEM((row, dk, dv), BF),
            pltpu.VMEM((4, cols, quarter), BF),
            pltpu.VMEM((4, ny, nz, 2, cols, quarter), BF),
            pltpu.VMEM((length, heads * dv), F32),
            pltpu.VMEM((length, heads * dv), BF),
            pltpu.VMEM(w_in.shape, BF),
            pltpu.VMEM(w_out.shape, BF),
            pltpu.VMEM(rows, BF),
            pltpu.VMEM(rows, BF),
            pltpu.VMEM(rows, BF),
            pltpu.VMEM(rows, BF),
            dma,
            dma,
            dma,
            dma,
            dma,
            dma,
            dma,
            dma((2,)),
            dma((2, 2, steps)),
            dma((2, 2, steps)),
            dma,
            dma,
            dma,
            dma((GROUPS,)),
            dma,
            dma,
            dma((2,)),
        ],
        compiler_params=pltpu.CompilerParams(
            collective_id=0, has_side_effects=True, vmem_limit_bytes=40 * 2**20
        ),
        name="layer",
    )(q, k, v, res, wt, w_in, w_out, ids, gates)


def solution(mesh, ny=8, nz=8, heads=16, dk=64, dv=128):
    def per_device(q, k, v, res, w, w_in, w_out, ids, gates):
        return layer(
            ny, nz, heads, dk, dv, q, k, v, res, w.T, w_in[0], w_out[0], ids.T, gates.T
        )

    tokens = P(("win", "seq"), None)
    experts = P("seq", None, None)
    return jax.shard_map(
        per_device,
        mesh=mesh,
        in_specs=(tokens,) * 4 + (P(None, "seq"), experts, experts, tokens, tokens),
        out_specs=tokens,
        check_vma=False,
    )
```

time: 406 us -> 116 us (0.29)
  waiting for transfers between devices: 257 us -> 0 us
  Pallas kernels: 0 us -> 106 us
  blocking collectives: 93 us -> 0 us
  between operations: 13.6 us -> 0.02 us
  matrix products: 11.6 us -> 0 us
  starting transfers between devices: 7.94 us -> 0 us
  local copies, waits for them, and re-layouts: 14.1 us -> 9.25 us
    all_gather x2 -> x0, waiting for transfers between devices: 227 us -> none  [the longest x1 144 us: carried_in(): gathered = lax.all_gather(x.astype(jnp.bfloat16), axis)]
    pallas_call x0 -> x1, Pallas kernels: none -> 106 us  [layer(): pl.pallas_call(functools.partial(layer_kernel, ny, nz, heads, dk, dv), ou...]
    all_to_all x1 -> x0, blocking collectives: 93 us -> none  [per_device(): lax.all_to_all(buffer, 'seq', split_axis=0, concat_axis=1, tiled=True)]
    all_to_all x1 -> x0, waiting for transfers between devices: 29.9 us -> none  [per_device(): lax.all_to_all(produced_all, 'seq', split_axis=1, concat_axis=0, tiled=True)]
    dot_general x6 -> x0, matrix products: 11.6 us -> none  [the longest x1 3.96 us: per_device(): jnp.dot(attended, lax.all_gather(out_weight, 'seq', axis=1, tiled=True),...]
    all_to_all x1 -> x0, starting transfers between devices: 7.9 us -> none  [per_device(): lax.all_to_all(produced_all, 'seq', split_axis=1, concat_axis=0, tiled=True)]
    unnamed x15 -> x19, local copies, waits for them, and re-layouts: 1.67 us -> 9.25 us
  transfers between devices with their start and end apart: 3 -> 0, of which waited for: 3 -> 0; matrix products, arithmetic and copies ran while one was open for 2% -> 0% of each run, Pallas kernels for 0% -> 0%
where the time goes in v1:
time: 116 us; the launch traced here: 115 us
  Pallas kernels  106 us (91%)
  local copies, waits for them, and re-layouts  9.25 us (8%)
    pallas_call x1, Pallas kernels, layer(): pl.pallas_call(functools.partial(layer_kernel, ny, nz, heads, dk, dv), ou...  106 us
    unnamed x19, local copies, waits for them, and re-layouts  9.25 us

profile of v1, /device:TPU:1, one launch (start us, length us, event | category | flops | bytes accessed | tf_op | source)
XLA Modules:
  0.0 115.0 jit_solution(9906711604898054378)
XLA Ops:
  0.0 0.0 copy-start
  0.0 1.4 %copy-done = bf16[1,1024,768]{2,1,0:T(8,128)(2,1)S(1)} copy-done((bf16[1,1024,768]{2,1,0:T(8,128)(2,1)S(1)}, bf16[1,1024,768]{2,1,0:T(8,128)(2,1)}, u32[]{:S(2)}) %copy-start) | copy-done | bytes 1572888
  1.4 0.0 copy-start.1
  1.4 1.1 copy-done.1
  2.5 0.0 copy-start.2
  2.5 1.0 copy-done.2
  3.6 0.0 copy-start.3
  3.6 0.9 copy-done.3
  4.5 0.0 copy-start.4
  4.5 0.9 copy-done.4
  5.5 0.0 copy-start.5
  5.5 0.9 copy-done.5
  6.4 0.0 copy-start.6
  6.4 0.8 copy-done.6
  7.2 0.0 copy-start.7
  7.2 0.7 copy-done.7
  7.9 0.0 copy-start.8
  7.9 0.7 copy-done.8
  8.6 105.7 %layer.1 = bf16[128,1024]{1,0:T(8,128)(2,1)S(1)} custom-call(bf16[128,1024]{1,0:T(8,128)(2,1)S(1)} %copy-done.3, bf16[128,1024]{1,0:T(8,128)(2,1)S(1)} %copy-done.4, bf16[128,2048]{1,0:T(8,128)(2,1)S(1)} %copy-done.2, bf16[128,1024]{1,0:T(8,128)(2,1)S(1)} %copy-done.5, bf16[8,2048]{1,0:T(8,128)(2,1)S(1)} %bitcast.7, bf16[1024,768]{1,0:T(8,128)(2,1)S(1)} %bitcast.5, ...), custom_call_target="tpu_custom_call" | custom-call | tf_op jit(solution)/shard_map/layer/pallas_call | solution.py:439
  114.3 0.7 copy.11
Async XLA Ops:
  0.0 1.4 %copy-start = (bf16[1,1024,768]{2,1,0:T(8,128)(2,1)S(1)}, bf16[1,1024,768]{2,1,0:T(8,128)(2,1)}, u32[]{:S(2)}) copy-start(bf16[1,1024,768]{2,1,0:T(8,128)(2,1)} %param.14) | copy-start | bytes 4718596
  1.4 1.1 copy-start.1
  2.5 1.0 copy-start.2
  3.6 0.9 copy-start.3
  4.5 0.9 copy-start.4
  5.5 0.9 copy-start.5
  6.4 0.8 copy-start.6
  7.2 0.7 copy-start.7
  7.9 0.7 copy-start.8

commit v2 on v1

v2 whole, which is shorter than its diff:
```python
import functools

import jax
import jax.numpy as jnp
from jax import lax
from jax.experimental import pallas as pl
from jax.experimental.pallas import tpu as pltpu
from jax.sharding import PartitionSpec as P

TOP = 2
CAP = 4
GROUPS = 4
MESH = pl.DeviceIdType.MESH
BF = jnp.bfloat16
F32 = jnp.float32


def dot(a, b, dims=((1,), (0,))):
    return lax.dot_general(a, b, (dims, ((), ())), preferred_element_type=F32)


def layer_kernel(
    ny,
    nz,
    heads,
    dk,
    dv,
    q_hbm,
    k_hbm,
    v_hbm,
    res_hbm,
    wt_hbm,
    win_hbm,
    wout_hbm,
    ids_hbm,
    gates_hbm,
    o_ref,
    q_ref,
    k_ref,
    v_ref,
    res_ref,
    wt_ref,
    ids_ref,
    gates_ref,
    s_loc,
    s_sib,
    s_pair,
    s_pair_out,
    tot,
    p_out,
    r1,
    r2,
    r3,
    prefix,
    w_loc,
    w_all,
    intra,
    attended,
    win,
    wout,
    xb,
    xr,
    yb,
    ret,
    s0_send,
    s0_recv,
    s1_send,
    s1_recv,
    s2_send,
    s2_recv,
    s3_send,
    s3_recv,
    s4_send,
    s4_recv,
    w0_send,
    w0_recv,
    w1_send,
    w1_recv,
    met,
    ring_send,
    ring_recv,
    sib_send,
    sib_recv,
    x_send,
    x_recv,
    y_send,
    y_recv,
    win_sem,
):
    n = ny * nz * 2
    row = nz * 2
    length = q_ref.shape[0]
    width = res_ref.shape[1]
    he = wout.shape[0]
    quarter = w_loc.shape[2]
    me = lax.axis_index("seq")
    y, z, c = me // row, lax.rem(me // 2, nz), lax.rem(me, 2)

    def seq(yy, zz, cc):
        return yy * row + zz * 2 + cc

    def remote(src, dst, ssem, rsem, dev):
        return pltpu.make_async_remote_copy(
            src_ref=src,
            dst_ref=dst,
            send_sem=ssem,
            recv_sem=rsem,
            device_id={"seq": dev},
            device_id_type=MESH,
        )

    def drain(ref, sem):
        pltpu.make_async_copy(ref, ref, sem).wait()

    loads = [
        pltpu.make_async_copy(src, dst, win_sem.at[i])
        for i, (src, dst) in enumerate(
            (
                (k_hbm, k_ref),
                (v_hbm, v_ref),
                (wt_hbm, wt_ref),
                (q_hbm, q_ref),
                (ids_hbm, ids_ref),
                (gates_hbm, gates_ref),
                (res_hbm, res_ref),
                (win_hbm, win),
                (wout_hbm, wout),
            )
        )
    ]
    for load in loads:
        load.start()
    barrier = pltpu.get_barrier_semaphore()

    def greet(dev):
        pl.semaphore_signal(barrier, inc=1, device_id={"seq": dev}, device_id_type=MESH)

    def greet_row(i, _):
        greet(seq(y, lax.rem(z + i, nz), c))
        return 0

    def greet_column(i, _):
        greet(seq(lax.rem(y + i, ny), z, c))
        return 0

    sib = seq(y, z, 1 - c)
    greet(sib)
    lax.fori_loop(1, nz, greet_row, 0)
    lax.fori_loop(1, ny, greet_column, 0)

    loads[0].wait()
    loads[1].wait()

    def states(p, _):
        kp = k_ref[:, pl.ds(pl.multiple_of(p * 2 * dk, 2 * dk), 2 * dk)]
        vp = v_ref[:, pl.ds(pl.multiple_of(p * 2 * dv, 2 * dv), 2 * dv)]
        kv = dot(kp, vp, ((0,), (0,)))
        s_loc[2 * p] = kv[:dk, :dv].astype(BF)
        s_loc[2 * p + 1] = kv[dk:, dv:].astype(BF)
        return 0

    lax.fori_loop(0, heads // 2, states, 0)
    loads[2].wait()
    for part in range(4):
        w_loc[part] = wt_ref[:, part * quarter : (part + 1) * quarter]

    pl.semaphore_wait(barrier, nz + ny - 1)

    hh = heads // 2
    own, other = c * hh, (1 - c) * hh
    pa, pb = 2 * c, 2 * c + 1
    first_core = c == 0
    remote(s_loc.at[pl.ds(other, hh)], s_sib, s0_send, s0_recv, sib).start()

    def w_join(part, which):
        pltpu.make_async_copy(
            w_loc.at[part], w_all.at[part, y, z, c], w0_recv.at[which]
        ).start()

    for which in range(2):
        part = 2 * (1 - c) + which
        remote(
            w_loc.at[part], w_all.at[part, y, z, c], w0_send, w0_recv.at[which], sib
        ).start()
    w_join(pa, 0)
    w_join(pb, 1)

    def tell(cc, yy):
        pl.semaphore_signal(
            met, inc=1, device_id={"seq": seq(yy, z, cc)}, device_id_type=MESH
        )

    def tell_column(i, _):
        tell(c, lax.rem(y + i, ny))
        return 0

    lax.fori_loop(1, ny, tell_column, 0)

    drain(s_sib, s0_recv)
    for i in range(hh):
        both = s_loc[own + i].astype(F32) + s_sib[i].astype(F32)
        s_pair[i] = both.astype(BF)
    pltpu.make_async_copy(s_pair.at[z], r1.at[z], s1_recv).start()

    def phase1(i, _):
        to = lax.rem(z + i, nz)
        remote(s_pair.at[to], r1.at[z], s1_send, s1_recv, seq(y, to, c)).start()
        return 0

    lax.fori_loop(1, nz, phase1, 0)

    def along_z(i, _):
        ref = w_all.at[pa, y, z]
        remote(ref, ref, w1_send.at[0], w1_recv.at[0], seq(y, lax.rem(z + i, nz), c)).start()
        return 0

    def along_y(i, _):
        ref = w_all.at[pb, y, z]
        remote(ref, ref, w1_send.at[1], w1_recv.at[1], seq(lax.rem(y + i, ny), z, c)).start()
        return 0

    drain(w_all.at[pa, y, z], w0_recv.at[0])
    lax.fori_loop(1, nz, along_z, 0)
    drain(w_all.at[pb, y, z], w0_recv.at[1])
    lax.fori_loop(1, ny, along_y, 0)

    t_row = lax.broadcasted_iota(jnp.int32, (2 * length, length), 0)
    t_col = lax.broadcasted_iota(jnp.int32, (2 * length, length), 1)
    causal = lax.rem(t_row, length) >= t_col
    first = lax.broadcasted_iota(jnp.int32, (length, 2 * dk), 1) < dk

    def two_heads(p):
        qp = q_ref[:, pl.ds(pl.multiple_of(p * 2 * dk, 2 * dk), 2 * dk)]
        zero = jnp.zeros_like(qp)
        return jnp.concatenate(
            [jnp.where(first, qp, zero), jnp.where(first, zero, qp)], axis=0
        )

    def inside(p, _):
        kp = k_ref[:, pl.ds(pl.multiple_of(p * 2 * dk, 2 * dk), 2 * dk)]
        at = pl.multiple_of(p * 2 * dv, 2 * dv)
        scores = dot(two_heads(p), kp, ((1,), (1,)))
        scores = jnp.where(causal, scores, 0.0).astype(BF)
        vp = v_ref[:, pl.ds(at, 2 * dv)]
        intra[:, pl.ds(at, dv)] = dot(scores[:length], vp[:, :dv])
        intra[:, pl.ds(pl.multiple_of(at + dv, dv), dv)] = dot(scores[length:], vp[:, dv:])
        return 0

    loads[3].wait()
    half = heads // 4
    lax.fori_loop(0, half, inside, 0)

    drain(r1, s1_recv)
    total = r1[0].astype(F32)
    for i in range(1, nz):
        total = total + r1[i].astype(F32)
    tot[...] = total.astype(BF)
    pltpu.make_async_copy(tot, r2.at[y], s2_recv).start()

    def phase2(i, _):
        yy = lax.rem(y + i, ny)
        remote(tot, r2.at[y], s2_send, s2_recv, seq(yy, z, c)).start()
        return 0

    lax.fori_loop(1, ny, phase2, 0)

    def mod_y(v):
        return lax.rem(v + 2 * ny, ny)

    def mod_z(v):
        return lax.rem(v + 2 * nz, nz)

    def piece(axis, origin, h):
        if axis == 0:
            return w_all.at[pa, origin, pl.ds(h * (nz // 2), nz // 2)]
        return w_all.at[pb, pl.ds(h * (ny // 2), ny // 2), origin]

    def pieces(axis, way, step):
        size = ny if axis == 0 else nz
        if 2 * step > size:
            return ()
        return (way,) if 2 * step == size else (way, 1 - way)

    def to_sibling(ref):
        remote(ref, ref, sib_send, sib_recv, sib).start()

    def ring_copy(axis, way, step, h):
        mod, at = (mod_y, y) if axis == 0 else (mod_z, z)
        sign = 1 if way == 0 else -1
        ref = piece(axis, mod(at - sign * (step - 1)), h)
        dev = seq(mod(at + sign), z, c) if axis == 0 else seq(y, mod(at + sign), c)
        place = (axis, way, step - 1, h)
        return remote(ref, ref, ring_send.at[place], ring_recv.at[place], dev)

    def ring_step(axis, step):
        mod, at = (mod_y, y) if axis == 0 else (mod_z, z)
        for turn in range(2):
            for way in (0, 1):
                if turn < len(pieces(axis, way, step)):
                    h = pieces(axis, way, step)[turn]
                    ref = piece(axis, mod(at - step if way == 0 else at + step), h)
                    drain(ref, ring_recv.at[axis, way, step - 1, h])
                    if h in pieces(axis, way, step + 1):
                        ring_copy(axis, way, step + 1, h).start()
                    to_sibling(ref)

    def ring_open(axis):
        for turn in range(2):
            for way in (0, 1):
                if turn < len(pieces(axis, way, 1)):
                    ring_copy(axis, way, 1, pieces(axis, way, 1)[turn]).start()

    drain(w_all.at[pa, y, pl.ds(0, nz - 1)], w1_recv.at[0])
    ring_open(0)
    drain(w_all.at[pb, pl.ds(0, ny - 1), z], w1_recv.at[1])
    ring_open(1)
    to_sibling(w_all.at[pa, y])
    to_sibling(w_all.at[pb, :, z])

    drain(r2, s2_recv)
    run = jnp.zeros(total.shape, F32)
    for yy in range(ny):
        run = run + jnp.where(yy < y, r2[yy].astype(F32), 0.0)
    for i in range(nz):
        p_out[i] = run.astype(BF)
        if i < nz - 1:
            run = run + r1[i].astype(F32)
    pltpu.make_async_copy(p_out.at[z], r3.at[z], s3_recv).start()

    def phase3(i, _):
        to = lax.rem(z + i, nz)
        remote(p_out.at[to], r3.at[z], s3_send, s3_recv, seq(y, to, c)).start()
        return 0

    lax.fori_loop(1, nz, phase3, 0)

    for axis in (0, 1):
        ring_step(axis, 1)
    lax.fori_loop(half, heads // 2, inside, 0)

    drain(r3, s3_recv)
    for i in range(hh):
        chip = r3[i].astype(F32)
        theirs = chip + jnp.where(first_core, s_loc[own + i].astype(F32), 0.0)
        s_pair_out[i] = theirs.astype(BF)
    remote(s_pair_out, prefix.at[pl.ds(own, hh)], s4_send, s4_recv, sib).start()
    for i in range(hh):
        chip = r3[i].astype(F32)
        mine = chip + jnp.where(first_core, 0.0, s_sib[i].astype(F32))
        prefix[own + i] = mine.astype(BF)

    for axis in (0, 1):
        ring_step(axis, 2)

    eye = lax.broadcasted_iota(jnp.int32, (length, length), 0) == lax.broadcasted_iota(
        jnp.int32, (length, length), 1
    )
    below = lax.broadcasted_iota(jnp.int32, (length, length), 1) < lax.broadcasted_iota(
        jnp.int32, (length, length), 0
    )
    above = lax.broadcasted_iota(jnp.int32, (length, length), 0) < lax.broadcasted_iota(
        jnp.int32, (length, length), 1
    )

    for load in loads[4:7]:
        load.wait()

    def column(r):
        return jnp.sum(jnp.where(eye, r, 0.0), axis=1, keepdims=True)

    id_row = [ids_ref[j : j + 1, :].astype(F32) for j in range(TOP)]
    id_col = [column(r) for r in id_row]
    gate_col = [column(gates_ref[j : j + 1, :]) for j in range(TOP)]
    place_row, place_col = [], []
    for j in range(TOP):
        row_count, col_count = 0.0, 0.0
        for i in range(TOP):
            row_count = row_count + jnp.where(above & (id_col[i] == id_row[j]), 1.0, 0.0)
            col_count = col_count + jnp.where(below & (id_col[j] == id_row[i]), 1.0, 0.0)
        place_row.append(id_row[j] * CAP + jnp.sum(row_count, axis=0, keepdims=True))
        place_col.append(id_col[j] * CAP + jnp.sum(col_count, axis=1, keepdims=True))
    rows = n * CAP
    r_iota = lax.broadcasted_iota(jnp.int32, (rows, length), 0).astype(F32)
    spread = jnp.where(
        (r_iota == place_row[0]) | (r_iota == place_row[1]), 1.0, 0.0
    ).astype(BF)

    position = me * length + lax.broadcasted_iota(jnp.int32, (length, 1), 0)
    scaling = lax.rsqrt((position.astype(F32) + 1.0) * dk)

    def before(p):
        past = prefix[pl.ds(2 * p, 2)].reshape(2 * dk, dv)
        earlier = dot(two_heads(p), past)
        for h in range(2):
            cols = pl.ds(pl.multiple_of((2 * p + h) * dv, dv), dv)
            attended[:, cols] = (
                (intra[:, cols] + earlier[h * length : (h + 1) * length]) * scaling
            ).astype(BF)

    for p in range(hh // 2):
        before(own // 2 + p)
    drain(prefix.at[pl.ds(other, hh)], s4_recv)
    for p in range(hh // 2):
        before(other // 2 + p)

    for step in range(3, max(ny, nz) // 2 + 1):
        for axis in (0, 1):
            ring_step(axis, step)

    def project(part):
        cols = pl.ds(pl.multiple_of(part * quarter, quarter), quarter)
        return dot(attended[:, cols], w_all[part].reshape(width, quarter), ((1,), (1,)))

    projected = project(pa) + project(pb)
    drain(w_all.at[pl.ds(2 * (1 - c), 2)], sib_recv)
    projected = projected + (project(2 * (1 - c)) + project(2 * (1 - c) + 1))
    hidden = (res_ref[...].astype(F32) + projected).astype(BF)
    hidden_float = hidden.astype(F32)
    intra[:, :width] = hidden_float
    normed = (
        hidden_float
        * lax.rsqrt(jnp.mean(hidden_float * hidden_float, axis=-1, keepdims=True) + 1e-06)
    ).astype(BF)
    xb[...] = dot(spread, normed).astype(BF).reshape(n, CAP, width)

    def offset(i):
        j = lax.rem(i * 37, n)
        return j // row, lax.rem(j // 2, nz), lax.rem(j, 2)

    def ahead(i):
        dy, dz, dc = offset(i)
        return seq(lax.rem(y + dy, ny), lax.rem(z + dz, nz), lax.rem(c + dc, 2))

    def behind(i):
        dy, dz, dc = offset(i)
        return seq(lax.rem(y - dy + ny, ny), lax.rem(z - dz + nz, nz), lax.rem(c - dc + 2, 2))

    per = n // GROUPS
    pl.semaphore_wait(met, ny - 1)
    pltpu.make_async_copy(xb.at[me], xr.at[0], x_recv.at[0]).start()

    def dispatch(i, _):
        to = ahead(i)
        remote(xb.at[to], xr.at[i], x_send, x_recv.at[i // per], to).start()
        return 0

    lax.fori_loop(1, n, dispatch, 0)

    loads[7].wait()
    loads[8].wait()

    def expert(g):
        lo = g * per
        drain(xr.at[pl.ds(lo, per)], x_recv.at[g])
        x = xr[pl.ds(lo, per)].reshape(per * CAP, width)
        act = dot(x, win[...])
        gate, up = act[:, :he], act[:, he:]
        inner = (gate / (1.0 + jnp.exp(-gate)) * up).astype(BF)
        yb[pl.ds(lo, per)] = dot(inner, wout[...]).astype(BF).reshape(per, CAP, width)

    def give_back(i, _):
        to = behind(i)
        remote(yb.at[i], ret.at[me], y_send, y_recv, to).start()
        return 0

    expert(0)
    pltpu.make_async_copy(yb.at[0], ret.at[me], y_recv).start()
    lax.fori_loop(1, per, give_back, 0)

    def group(g, _):
        expert(g)
        lax.fori_loop(g * per, (g + 1) * per, give_back, 0)
        return 0

    lax.fori_loop(1, GROUPS, group, 0)

    r_lane = lax.broadcasted_iota(jnp.int32, (length, rows), 1).astype(F32)
    picks = [jnp.where(r_lane == place_col[j], 1.0, 0.0).astype(BF) for j in range(TOP)]
    drain(ret, y_recv)
    back = ret[...].reshape(rows, width)
    combined = dot(picks[0], back) * gate_col[0] + dot(picks[1], back) * gate_col[1]
    o_ref[...] = (intra[:, :width] + combined).astype(BF)

    drain(s_sib, s0_send)
    drain(r1.at[pl.ds(0, nz - 1)], s1_send)
    drain(r2.at[pl.ds(0, ny - 1)], s2_send)
    drain(r3.at[pl.ds(0, nz - 1)], s3_send)
    drain(s_sib, s4_send)
    drain(w_loc.at[pl.ds(0, 2)], w0_send)
    drain(w_all.at[pa, y, pl.ds(0, nz - 1)], w1_send.at[0])
    drain(w_all.at[pb, pl.ds(0, ny - 1), z], w1_send.at[1])
    for axis in (0, 1):
        for step in range(1, max(ny, nz) // 2 + 1):
            for way in (0, 1):
                for h in pieces(axis, way, step):
                    ring_copy(axis, way, step, h).wait_send()
    drain(w_all.at[pl.ds(2 * c, 2)], sib_send)
    drain(xb.at[pl.ds(0, n - 1)], x_send)
    drain(yb.at[pl.ds(0, n - 1)], y_send)


def layer(ny, nz, heads, dk, dv, q, k, v, res, wt, w_in, w_out, ids, gates):
    n = ny * nz * 2
    length, width = res.shape
    cols = wt.shape[0]
    quarter = heads * dv // 4
    vmem = pl.BlockSpec(memory_space=pltpu.VMEM)
    hbm = pl.BlockSpec(memory_space=pl.ANY)
    steps = max(ny, nz) // 2
    dma = pltpu.SemaphoreType.DMA
    rows = (n, CAP, width)
    return pl.pallas_call(
        functools.partial(layer_kernel, ny, nz, heads, dk, dv),
        out_shape=jax.ShapeDtypeStruct((length, width), BF),
        in_specs=[hbm] * 9,
        out_specs=vmem,
        scratch_shapes=[
            *[pltpu.VMEM(a.shape, a.dtype) for a in (q, k, v, res, wt, ids, gates)],
            pltpu.VMEM((heads, dk, dv), BF),
            pltpu.VMEM((nz, dk, dv), BF),
            pltpu.VMEM((nz, dk, dv), BF),
            pltpu.VMEM((nz, dk, dv), BF),
            pltpu.VMEM((dk, dv), BF),
            pltpu.VMEM((nz, dk, dv), BF),
            pltpu.VMEM((nz, dk, dv), BF),
            pltpu.VMEM((ny, dk, dv), BF),
            pltpu.VMEM((nz, dk, dv), BF),
            pltpu.VMEM((heads, dk, dv), BF),
            pltpu.VMEM((4, cols, quarter), BF),
            pltpu.VMEM((4, ny, nz, 2, cols, quarter), BF),
            pltpu.VMEM((length, heads * dv), F32),
            pltpu.VMEM((length, heads * dv), BF),
            pltpu.VMEM(w_in.shape, BF),
            pltpu.VMEM(w_out.shape, BF),
            pltpu.VMEM(rows, BF),
            pltpu.VMEM(rows, BF),
            pltpu.VMEM(rows, BF),
            pltpu.VMEM(rows, BF),
            *[dma] * 11,
            dma((2,)),
            dma((2,)),
            dma((2,)),
            pltpu.SemaphoreType.REGULAR,
            dma((2, 2, steps, 2)),
            dma((2, 2, steps, 2)),
            dma,
            dma,
            dma,
            dma((GROUPS,)),
            dma,
            dma,
            dma((9,)),
        ],
        compiler_params=pltpu.CompilerParams(
            collective_id=0, has_side_effects=True, vmem_limit_bytes=60 * 2**20
        ),
        name="layer",
    )(q, k, v, res, wt, w_in, w_out, ids, gates)


def solution(mesh, ny=8, nz=8, heads=16, dk=64, dv=128):
    def per_device(q, k, v, res, w, w_in, w_out, ids, gates):
        return layer(
            ny, nz, heads, dk, dv, q, k, v, res, w.T, w_in[0], w_out[0], ids.T, gates.T
        )

    tokens = P(("win", "seq"), None)
    experts = P("seq", None, None)
    return jax.shard_map(
        per_device,
        mesh=mesh,
        in_specs=(tokens,) * 4 + (P(None, "seq"), experts, experts, tokens, tokens),
        out_specs=tokens,
        check_vma=False,
    )
```

time: 116 us -> 99.6 us (0.86)
  Pallas kernels: 106 us -> 97.8 us
  local copies, waits for them, and re-layouts: 9.25 us -> 1.67 us
    pallas_call x1, Pallas kernels: 106 us -> 97.8 us  [layer(): pl.pallas_call(functools.partial(layer_kernel, ny, nz, heads, dk, dv), ou...]
    unnamed x19 -> x1, local copies, waits for them, and re-layouts: 9.25 us -> 1.67 us
where the time goes in v2:
time: 99.6 us; the launch traced here: 99.5 us
  Pallas kernels  97.8 us (98%)
  local copies, waits for them, and re-layouts  1.67 us (2%)
    pallas_call x1, Pallas kernels, layer(): pl.pallas_call(functools.partial(layer_kernel, ny, nz, heads, dk, dv), ou...  97.8 us

profile of v2, /device:TPU:1, one launch (start us, length us, event | category | flops | bytes accessed | tf_op | source)
XLA Modules:
  0.0 99.5 jit_solution(1365592513595483431)
XLA Ops:
  0.0 97.8 %layer.1 = bf16[128,1024]{1,0:T(8,128)(2,1)} custom-call(bf16[128,1024]{1,0:T(8,128)(2,1)} %q_hbm.1, bf16[128,1024]{1,0:T(8,128)(2,1)} %k_hbm.1, bf16[128,2048]{1,0:T(8,128)(2,1)} %v_hbm.1, bf16[128,1024]{1,0:T(8,128)(2,1)} %res_hbm.1, bf16[8,2048]{1,0:T(8,128)(2,1)} %bitcast.7, bf16[1024,768]{1,0:T(8,128)(2,1)} %bitcast.5, bf16[384,1024]{1,0:T(8,128)(2,1)} %bitcast.6, ...), custom_call_target="tpu_custom_call" | custom-call | tf_op jit(solution)/shard_map/layer/pallas_call | solution.py:512
  97.8 1.7 %copy.11 = bf16[128,1024]{1,0:T(8,128)(2,1)} copy(bf16[128,1024]{1,0:T(8,128)(2,1)} %layer.1) | data formatting | bytes 524288

commit v3 on v2

--- a/solution.py
+++ b/solution.py
@@ -72,8 +72,6 @@
     s3_recv,
     s4_send,
     s4_recv,
-    w0_send,
-    w0_recv,
     w1_send,
     w1_recv,
     met,
@@ -93,8 +91,10 @@
     width = res_ref.shape[1]
     he = wout.shape[0]
     quarter = w_loc.shape[2]
+    cut = min(4, ny, nz)
     me = lax.axis_index("seq")
     y, z, c = me // row, lax.rem(me // 2, nz), lax.rem(me, 2)
+    at_row = lax.rem(me, row)
 
     def seq(yy, zz, cc):
         return yy * row + zz * 2 + cc
@@ -136,54 +136,65 @@
         pl.semaphore_signal(barrier, inc=1, device_id={"seq": dev}, device_id_type=MESH)
 
     def greet_row(i, _):
-        greet(seq(y, lax.rem(z + i, nz), c))
+        greet(y * row + lax.rem(at_row + i, row))
         return 0
 
     def greet_column(i, _):
-        greet(seq(lax.rem(y + i, ny), z, c))
+        greet(seq(lax.rem(y + i // 2, ny), z, lax.rem(c + i, 2)))
         return 0
 
     sib = seq(y, z, 1 - c)
-    greet(sib)
-    lax.fori_loop(1, nz, greet_row, 0)
-    lax.fori_loop(1, ny, greet_column, 0)
-
-    loads[0].wait()
-    loads[1].wait()
-
-    def states(p, _):
-        kp = k_ref[:, pl.ds(pl.multiple_of(p * 2 * dk, 2 * dk), 2 * dk)]
-        vp = v_ref[:, pl.ds(pl.multiple_of(p * 2 * dv, 2 * dv), 2 * dv)]
-        kv = dot(kp, vp, ((0,), (0,)))
-        s_loc[2 * p] = kv[:dk, :dv].astype(BF)
-        s_loc[2 * p + 1] = kv[dk:, dv:].astype(BF)
-        return 0
-
-    lax.fori_loop(0, heads // 2, states, 0)
+    lax.fori_loop(1, row, greet_row, 0)
+    lax.fori_loop(2, 2 * ny, greet_column, 0)
+
     loads[2].wait()
     for part in range(4):
         w_loc[part] = wt_ref[:, part * quarter : (part + 1) * quarter]
-
-    pl.semaphore_wait(barrier, nz + ny - 1)
+    pl.semaphore_wait(barrier, row + 2 * ny - 3)
+
+    pa, pb = 2 * c, 2 * c + 1
+
+    def keep(part, sem):
+        pltpu.make_async_copy(w_loc.at[part], w_all.at[part, y, z, c], sem).start()
+
+    def along_z(i, _):
+        to = lax.rem(at_row + i, row)
+        part = 2 * lax.rem(to, 2)
+        remote(
+            w_loc.at[part], w_all.at[part, y, z, c], w1_send.at[0], w1_recv.at[0], y * row + to
+        ).start()
+        return 0
+
+    def along_y(i, _):
+        cc = lax.rem(c + i, 2)
+        part = 2 * cc + 1
+        remote(
+            w_loc.at[part],
+            w_all.at[part, y, z, c],
+            w1_send.at[1],
+            w1_recv.at[1],
+            seq(lax.rem(y + i // 2, ny), z, cc),
+        ).start()
+        return 0
+
+    keep(pa, w1_recv.at[0])
+    keep(pb, w1_recv.at[1])
+    lax.fori_loop(1, row, along_z, 0)
+    lax.fori_loop(1, 2 * ny, along_y, 0)
+
+    loads[0].wait()
+    loads[1].wait()
+
+    for p in range(heads // 2):
+        kp = k_ref[:, 2 * p * dk : 2 * (p + 1) * dk]
+        kv = dot(kp, v_ref[:, 2 * p * dv : 2 * (p + 1) * dv], ((0,), (0,)))
+        s_loc[2 * p] = kv[:dk, :dv].astype(BF)
+        s_loc[2 * p + 1] = kv[dk:, dv:].astype(BF)
 
     hh = heads // 2
     own, other = c * hh, (1 - c) * hh
-    pa, pb = 2 * c, 2 * c + 1
     first_core = c == 0
     remote(s_loc.at[pl.ds(other, hh)], s_sib, s0_send, s0_recv, sib).start()
-
-    def w_join(part, which):
-        pltpu.make_async_copy(
-            w_loc.at[part], w_all.at[part, y, z, c], w0_recv.at[which]
-        ).start()
-
-    for which in range(2):
-        part = 2 * (1 - c) + which
-        remote(
-            w_loc.at[part], w_all.at[part, y, z, c], w0_send, w0_recv.at[which], sib
-        ).start()
-    w_join(pa, 0)
-    w_join(pb, 1)
 
     def tell(cc, yy):
         pl.semaphore_signal(
@@ -195,162 +206,6 @@
         return 0
 
     lax.fori_loop(1, ny, tell_column, 0)
-
-    drain(s_sib, s0_recv)
-    for i in range(hh):
-        both = s_loc[own + i].astype(F32) + s_sib[i].astype(F32)
-        s_pair[i] = both.astype(BF)
-    pltpu.make_async_copy(s_pair.at[z], r1.at[z], s1_recv).start()
-
-    def phase1(i, _):
-        to = lax.rem(z + i, nz)
-        remote(s_pair.at[to], r1.at[z], s1_send, s1_recv, seq(y, to, c)).start()
-        return 0
-
-    lax.fori_loop(1, nz, phase1, 0)
-
-    def along_z(i, _):
-        ref = w_all.at[pa, y, z]
-        remote(ref, ref, w1_send.at[0], w1_recv.at[0], seq(y, lax.rem(z + i, nz), c)).start()
-        return 0
-
-    def along_y(i, _):
-        ref = w_all.at[pb, y, z]
-        remote(ref, ref, w1_send.at[1], w1_recv.at[1], seq(lax.rem(y + i, ny), z, c)).start()
-        return 0
-
-    drain(w_all.at[pa, y, z], w0_recv.at[0])
-    lax.fori_loop(1, nz, along_z, 0)
-    drain(w_all.at[pb, y, z], w0_recv.at[1])
-    lax.fori_loop(1, ny, along_y, 0)
-
-    t_row = lax.broadcasted_iota(jnp.int32, (2 * length, length), 0)
-    t_col = lax.broadcasted_iota(jnp.int32, (2 * length, length), 1)
-    causal = lax.rem(t_row, length) >= t_col
-    first = lax.broadcasted_iota(jnp.int32, (length, 2 * dk), 1) < dk
-
-    def two_heads(p):
-        qp = q_ref[:, pl.ds(pl.multiple_of(p * 2 * dk, 2 * dk), 2 * dk)]
-        zero = jnp.zeros_like(qp)
-        return jnp.concatenate(
-            [jnp.where(first, qp, zero), jnp.where(first, zero, qp)], axis=0
-        )
-
-    def inside(p, _):
-        kp = k_ref[:, pl.ds(pl.multiple_of(p * 2 * dk, 2 * dk), 2 * dk)]
-        at = pl.multiple_of(p * 2 * dv, 2 * dv)
-        scores = dot(two_heads(p), kp, ((1,), (1,)))
-        scores = jnp.where(causal, scores, 0.0).astype(BF)
-        vp = v_ref[:, pl.ds(at, 2 * dv)]
-        intra[:, pl.ds(at, dv)] = dot(scores[:length], vp[:, :dv])
-        intra[:, pl.ds(pl.multiple_of(at + dv, dv), dv)] = dot(scores[length:], vp[:, dv:])
-        return 0
-
-    loads[3].wait()
-    half = heads // 4
-    lax.fori_loop(0, half, inside, 0)
-
-    drain(r1, s1_recv)
-    total = r1[0].astype(F32)
-    for i in range(1, nz):
-        total = total + r1[i].astype(F32)
-    tot[...] = total.astype(BF)
-    pltpu.make_async_copy(tot, r2.at[y], s2_recv).start()
-
-    def phase2(i, _):
-        yy = lax.rem(y + i, ny)
-        remote(tot, r2.at[y], s2_send, s2_recv, seq(yy, z, c)).start()
-        return 0
-
-    lax.fori_loop(1, ny, phase2, 0)
-
-    def mod_y(v):
-        return lax.rem(v + 2 * ny, ny)
-
-    def mod_z(v):
-        return lax.rem(v + 2 * nz, nz)
-
-    def piece(axis, origin, h):
-        if axis == 0:
-            return w_all.at[pa, origin, pl.ds(h * (nz // 2), nz // 2)]
-        return w_all.at[pb, pl.ds(h * (ny // 2), ny // 2), origin]
-
-    def pieces(axis, way, step):
-        size = ny if axis == 0 else nz
-        if 2 * step > size:
-            return ()
-        return (way,) if 2 * step == size else (way, 1 - way)
-
-    def to_sibling(ref):
-        remote(ref, ref, sib_send, sib_recv, sib).start()
-
-    def ring_copy(axis, way, step, h):
-        mod, at = (mod_y, y) if axis == 0 else (mod_z, z)
-        sign = 1 if way == 0 else -1
-        ref = piece(axis, mod(at - sign * (step - 1)), h)
-        dev = seq(mod(at + sign), z, c) if axis == 0 else seq(y, mod(at + sign), c)
-        place = (axis, way, step - 1, h)
-        return remote(ref, ref, ring_send.at[place], ring_recv.at[place], dev)
-
-    def ring_step(axis, step):
-        mod, at = (mod_y, y) if axis == 0 else (mod_z, z)
-        for turn in range(2):
-            for way in (0, 1):
-                if turn < len(pieces(axis, way, step)):
-                    h = pieces(axis, way, step)[turn]
-                    ref = piece(axis, mod(at - step if way == 0 else at + step), h)
-                    drain(ref, ring_recv.at[axis, way, step - 1, h])
-                    if h in pieces(axis, way, step + 1):
-                        ring_copy(axis, way, step + 1, h).start()
-                    to_sibling(ref)
-
-    def ring_open(axis):
-        for turn in range(2):
-            for way in (0, 1):
-                if turn < len(pieces(axis, way, 1)):
-                    ring_copy(axis, way, 1, pieces(axis, way, 1)[turn]).start()
-
-    drain(w_all.at[pa, y, pl.ds(0, nz - 1)], w1_recv.at[0])
-    ring_open(0)
-    drain(w_all.at[pb, pl.ds(0, ny - 1), z], w1_recv.at[1])
-    ring_open(1)
-    to_sibling(w_all.at[pa, y])
-    to_sibling(w_all.at[pb, :, z])
-
-    drain(r2, s2_recv)
-    run = jnp.zeros(total.shape, F32)
-    for yy in range(ny):
-        run = run + jnp.where(yy < y, r2[yy].astype(F32), 0.0)
-    for i in range(nz):
-        p_out[i] = run.astype(BF)
-        if i < nz - 1:
-            run = run + r1[i].astype(F32)
-    pltpu.make_async_copy(p_out.at[z], r3.at[z], s3_recv).start()
-
-    def phase3(i, _):
-        to = lax.rem(z + i, nz)
-        remote(p_out.at[to], r3.at[z], s3_send, s3_recv, seq(y, to, c)).start()
-        return 0
-
-    lax.fori_loop(1, nz, phase3, 0)
-
-    for axis in (0, 1):
-        ring_step(axis, 1)
-    lax.fori_loop(half, heads // 2, inside, 0)
-
-    drain(r3, s3_recv)
-    for i in range(hh):
-        chip = r3[i].astype(F32)
-        theirs = chip + jnp.where(first_core, s_loc[own + i].astype(F32), 0.0)
-        s_pair_out[i] = theirs.astype(BF)
-    remote(s_pair_out, prefix.at[pl.ds(own, hh)], s4_send, s4_recv, sib).start()
-    for i in range(hh):
-        chip = r3[i].astype(F32)
-        mine = chip + jnp.where(first_core, 0.0, s_sib[i].astype(F32))
-        prefix[own + i] = mine.astype(BF)
-
-    for axis in (0, 1):
-        ring_step(axis, 2)
 
     eye = lax.broadcasted_iota(jnp.int32, (length, length), 0) == lax.broadcasted_iota(
         jnp.int32, (length, length), 1
@@ -385,6 +240,152 @@
         (r_iota == place_row[0]) | (r_iota == place_row[1]), 1.0, 0.0
     ).astype(BF)
 
+    drain(s_sib, s0_recv)
+    for i in range(hh):
+        both = s_loc[own + i].astype(F32) + s_sib[i].astype(F32)
+        s_pair[i] = both.astype(BF)
+    pltpu.make_async_copy(s_pair.at[z], r1.at[z], s1_recv).start()
+
+    def phase1(i, _):
+        to = lax.rem(z + i, nz)
+        remote(s_pair.at[to], r1.at[z], s1_send, s1_recv, seq(y, to, c)).start()
+        return 0
+
+    lax.fori_loop(1, nz, phase1, 0)
+
+    t_row = lax.broadcasted_iota(jnp.int32, (2 * length, length), 0)
+    t_col = lax.broadcasted_iota(jnp.int32, (2 * length, length), 1)
+    causal = lax.rem(t_row, length) >= t_col
+    first = lax.broadcasted_iota(jnp.int32, (length, 2 * dk), 1) < dk
+
+    def two_heads(p):
+        qp = q_ref[:, pl.ds(pl.multiple_of(p * 2 * dk, 2 * dk), 2 * dk)]
+        zero = jnp.zeros_like(qp)
+        return jnp.concatenate(
+            [jnp.where(first, qp, zero), jnp.where(first, zero, qp)], axis=0
+        )
+
+    def inside(p, _):
+        kp = k_ref[:, pl.ds(pl.multiple_of(p * 2 * dk, 2 * dk), 2 * dk)]
+        at = pl.multiple_of(p * 2 * dv, 2 * dv)
+        scores = dot(two_heads(p), kp, ((1,), (1,)))
+        scores = jnp.where(causal, scores, 0.0).astype(BF)
+        vp = v_ref[:, pl.ds(at, 2 * dv)]
+        intra[:, pl.ds(at, dv)] = dot(scores[:length], vp[:, :dv])
+        intra[:, pl.ds(pl.multiple_of(at + dv, dv), dv)] = dot(scores[length:], vp[:, dv:])
+        return 0
+
+    loads[3].wait()
+    half = heads // 4
+    lax.fori_loop(0, half, inside, 0)
+
+    def mod_y(v):
+        return lax.rem(v + 2 * ny, ny)
+
+    def mod_z(v):
+        return lax.rem(v + 2 * nz, nz)
+
+    def piece(axis, origin, h, many=1):
+        if axis == 0:
+            return w_all.at[pa, origin, pl.ds(h * (nz // cut), many * (nz // cut))]
+        return w_all.at[pb, pl.ds(h * (ny // cut), many * (ny // cut)), origin]
+
+    def pieces(axis, way, step):
+        size = ny if axis == 0 else nz
+        mine = tuple(range(way * cut // 2, (way + 1) * cut // 2))
+        if 2 * step > size:
+            return ()
+        return mine if 2 * step == size else mine + tuple(set(range(cut)) - set(mine))
+
+    def to_sibling(ref):
+        remote(ref, ref, sib_send, sib_recv, sib).start()
+
+    def ring_copy(axis, way, step, h):
+        mod, at = (mod_y, y) if axis == 0 else (mod_z, z)
+        sign = 1 if way == 0 else -1
+        ref = piece(axis, mod(at - sign * (step - 1)), h)
+        dev = seq(mod(at + sign), z, c) if axis == 0 else seq(y, mod(at + sign), c)
+        place = (axis, way, step - 1, h)
+        return remote(ref, ref, ring_send.at[place], ring_recv.at[place], dev)
+
+    def ring_step(step):
+        for turn in range(cut):
+            for axis in (0, 1):
+                mod, at = (mod_y, y) if axis == 0 else (mod_z, z)
+                for way in (0, 1):
+                    order = pieces(axis, way, step)
+                    if turn < len(order):
+                        h = order[turn]
+                        origin = mod(at - step if way == 0 else at + step)
+                        drain(piece(axis, origin, h), ring_recv.at[axis, way, step - 1, h])
+                        if h in pieces(axis, way, step + 1):
+                            ring_copy(axis, way, step + 1, h).start()
+                        if turn == len(order) - 1:
+                            to_sibling(piece(axis, origin, min(order), len(order)))
+
+    def ring_open(axis):
+        for turn in range(cut):
+            for way in (0, 1):
+                if turn < len(pieces(axis, way, 1)):
+                    ring_copy(axis, way, 1, pieces(axis, way, 1)[turn]).start()
+
+    drain(w_all.at[pa, y], w1_recv.at[0])
+    ring_open(0)
+    drain(w_all.at[pb, :, z], w1_recv.at[1])
+    ring_open(1)
+    to_sibling(w_all.at[pa, y])
+    to_sibling(w_all.at[pb, :, z])
+
+    lax.fori_loop(half, heads // 2, inside, 0)
+
+    drain(r1, s1_recv)
+    total = r1[0].astype(F32)
+    for i in range(1, nz):
+        total = total + r1[i].astype(F32)
+    tot[...] = total.astype(BF)
+    pltpu.make_async_copy(tot, r2.at[y], s2_recv).start()
+
+    def phase2(i, _):
+        yy = lax.rem(y + i, ny)
+        remote(tot, r2.at[y], s2_send, s2_recv, seq(yy, z, c)).start()
+        return 0
+
+    lax.fori_loop(1, ny, phase2, 0)
+
+    ring_step(1)
+
+    drain(r2, s2_recv)
+    run = jnp.zeros(total.shape, F32)
+    for yy in range(ny):
+        run = run + jnp.where(yy < y, r2[yy].astype(F32), 0.0)
+    for i in range(nz):
+        p_out[i] = run.astype(BF)
+        if i < nz - 1:
+            run = run + r1[i].astype(F32)
+    pltpu.make_async_copy(p_out.at[z], r3.at[z], s3_recv).start()
+
+    def phase3(i, _):
+        to = lax.rem(z + i, nz)
+        remote(p_out.at[to], r3.at[z], s3_send, s3_recv, seq(y, to, c)).start()
+        return 0
+
+    lax.fori_loop(1, nz, phase3, 0)
+
+    ring_step(2)
+
+    drain(r3, s3_recv)
+    for i in range(hh):
+        chip = r3[i].astype(F32)
+        theirs = chip + jnp.where(first_core, s_loc[own + i].astype(F32), 0.0)
+        s_pair_out[i] = theirs.astype(BF)
+    remote(s_pair_out, prefix.at[pl.ds(own, hh)], s4_send, s4_recv, sib).start()
+    for i in range(hh):
+        chip = r3[i].astype(F32)
+        mine = chip + jnp.where(first_core, 0.0, s_sib[i].astype(F32))
+        prefix[own + i] = mine.astype(BF)
+
+    ring_step(3)
+
     position = me * length + lax.broadcasted_iota(jnp.int32, (length, 1), 0)
     scaling = lax.rsqrt((position.astype(F32) + 1.0) * dk)
 
@@ -403,9 +404,8 @@
     for p in range(hh // 2):
         before(other // 2 + p)
 
-    for step in range(3, max(ny, nz) // 2 + 1):
-        for axis in (0, 1):
-            ring_step(axis, step)
+    for step in range(4, max(ny, nz) // 2 + 1):
+        ring_step(step)
 
     def project(part):
         cols = pl.ds(pl.multiple_of(part * quarter, quarter), quarter)
@@ -475,10 +475,13 @@
     lax.fori_loop(1, GROUPS, group, 0)
 
     r_lane = lax.broadcasted_iota(jnp.int32, (length, rows), 1).astype(F32)
-    picks = [jnp.where(r_lane == place_col[j], 1.0, 0.0).astype(BF) for j in range(TOP)]
+    picks = jnp.concatenate(
+        [jnp.where(r_lane == place_col[j], 1.0, 0.0).astype(BF) for j in range(TOP)], axis=0
+    )
     drain(ret, y_recv)
     back = ret[...].reshape(rows, width)
-    combined = dot(picks[0], back) * gate_col[0] + dot(picks[1], back) * gate_col[1]
+    picked = dot(picks, back)
+    combined = picked[:length] * gate_col[0] + picked[length:] * gate_col[1]
     o_ref[...] = (intra[:, :width] + combined).astype(BF)
 
     drain(s_sib, s0_send)
@@ -486,9 +489,10 @@
     drain(r2.at[pl.ds(0, ny - 1)], s2_send)
     drain(r3.at[pl.ds(0, nz - 1)], s3_send)
     drain(s_sib, s4_send)
-    drain(w_loc.at[pl.ds(0, 2)], w0_send)
-    drain(w_all.at[pa, y, pl.ds(0, nz - 1)], w1_send.at[0])
-    drain(w_all.at[pb, pl.ds(0, ny - 1), z], w1_send.at[1])
+    drain(w_all.at[0, 0, pl.ds(0, nz - 1)], w1_send.at[0])
+    drain(w_loc.at[0], w1_send.at[0])
+    drain(w_all.at[0, pl.ds(0, ny - 1), 0], w1_send.at[1])
+    drain(w_loc.at[0], w1_send.at[1])
     for axis in (0, 1):
         for step in range(1, max(ny, nz) // 2 + 1):
             for way in (0, 1):
@@ -536,13 +540,12 @@
             pltpu.VMEM(rows, BF),
             pltpu.VMEM(rows, BF),
             pltpu.VMEM(rows, BF),
-            *[dma] * 11,
-            dma((2,)),
+            *[dma] * 10,
             dma((2,)),
             dma((2,)),
             pltpu.SemaphoreType.REGULAR,
-            dma((2, 2, steps, 2)),
-            dma((2, 2, steps, 2)),
+            dma((2, 2, steps, 4)),
+            dma((2, 2, steps, 4)),
             dma,
             dma,
             dma,

time: 99.6 us -> 97.1 us (0.975)
  Pallas kernels: 97.8 us -> 95.2 us
    pallas_call x1, Pallas kernels: 97.8 us -> 95.2 us  [layer(): pl.pallas_call(functools.partial(layer_kernel, ny, nz, heads, dk, dv), ou...]
where the time goes in v3:
time: 97.1 us; the launch traced here: 96.9 us
  Pallas kernels  95.2 us (98%)
  local copies, waits for them, and re-layouts  1.67 us (2%)
    pallas_call x1, Pallas kernels, layer(): pl.pallas_call(functools.partial(layer_kernel, ny, nz, heads, dk, dv), ou...  95.2 us

profile of v3, /device:TPU:1, one launch (start us, length us, event | category | flops | bytes accessed | tf_op | source)
XLA Modules:
  0.0 96.9 jit_solution(15340911102056211599)
XLA Ops:
  0.0 95.2 %layer.1 = bf16[128,1024]{1,0:T(8,128)(2,1)} custom-call(bf16[128,1024]{1,0:T(8,128)(2,1)} %q_hbm.1, bf16[128,1024]{1,0:T(8,128)(2,1)} %k_hbm.1, bf16[128,2048]{1,0:T(8,128)(2,1)} %v_hbm.1, bf16[128,1024]{1,0:T(8,128)(2,1)} %res_hbm.1, bf16[8,2048]{1,0:T(8,128)(2,1)} %bitcast.7, bf16[1024,768]{1,0:T(8,128)(2,1)} %bitcast.5, bf16[384,1024]{1,0:T(8,128)(2,1)} %bitcast.6, ...), custom_call_target="tpu_custom_call" | custom-call | tf_op jit(solution)/shard_map/layer/pallas_call | solution.py:516
  95.3 1.7 %copy.11 = bf16[128,1024]{1,0:T(8,128)(2,1)} copy(bf16[128,1024]{1,0:T(8,128)(2,1)} %layer.1) | data formatting | bytes 524288

commit v4 on v3

--- a/solution.py
+++ b/solution.py
@@ -58,6 +58,7 @@
     attended,
     win,
     wout,
+    spread,
     xb,
     xr,
     yb,
@@ -90,8 +91,8 @@
     length = q_ref.shape[0]
     width = res_ref.shape[1]
     he = wout.shape[0]
-    quarter = w_loc.shape[2]
-    cut = min(4, ny, nz)
+    part = w_loc.shape[2]
+    cut = min(4, nz)
     me = lax.axis_index("seq")
     y, z, c = me // row, lax.rem(me // 2, nz), lax.rem(me, 2)
     at_row = lax.rem(me, row)
@@ -148,40 +149,27 @@
     lax.fori_loop(2, 2 * ny, greet_column, 0)
 
     loads[2].wait()
-    for part in range(4):
-        w_loc[part] = wt_ref[:, part * quarter : (part + 1) * quarter]
+    for h in range(2):
+        w_loc[h] = wt_ref[:, h * part : (h + 1) * part]
     pl.semaphore_wait(barrier, row + 2 * ny - 3)
 
-    pa, pb = 2 * c, 2 * c + 1
-
-    def keep(part, sem):
-        pltpu.make_async_copy(w_loc.at[part], w_all.at[part, y, z, c], sem).start()
+    ring_at = y + c * (z - y)
 
     def along_z(i, _):
-        to = lax.rem(at_row + i, row)
-        part = 2 * lax.rem(to, 2)
-        remote(
-            w_loc.at[part], w_all.at[part, y, z, c], w1_send.at[0], w1_recv.at[0], y * row + to
-        ).start()
+        to = lax.rem(z + i, nz)
+        remote(w_loc.at[0], w_all.at[0, y, z, c], w1_send, w1_recv, seq(y, to, 0)).start()
         return 0
 
     def along_y(i, _):
-        cc = lax.rem(c + i, 2)
-        part = 2 * cc + 1
-        remote(
-            w_loc.at[part],
-            w_all.at[part, y, z, c],
-            w1_send.at[1],
-            w1_recv.at[1],
-            seq(lax.rem(y + i // 2, ny), z, cc),
-        ).start()
-        return 0
-
-    keep(pa, w1_recv.at[0])
-    keep(pb, w1_recv.at[1])
-    lax.fori_loop(1, row, along_z, 0)
-    lax.fori_loop(1, 2 * ny, along_y, 0)
-
+        to = lax.rem(y + i, ny)
+        remote(w_loc.at[1], w_all.at[1, z, y, c], w1_send, w1_recv, seq(to, z, 1)).start()
+        return 0
+
+    pltpu.make_async_copy(
+        w_loc.at[c], w_all.at[c, ring_at, y + z - ring_at, c], w1_recv
+    ).start()
+    lax.fori_loop(1 - c, nz, along_z, 0)
+    lax.fori_loop(c, ny, along_y, 0)
     loads[0].wait()
     loads[1].wait()
 
@@ -223,7 +211,13 @@
     def column(r):
         return jnp.sum(jnp.where(eye, r, 0.0), axis=1, keepdims=True)
 
-    id_row = [ids_ref[j : j + 1, :].astype(F32) for j in range(TOP)]
+    def turn_of(e):
+        dy = ((e >> (row.bit_length() - 1)) + (ny - y)) & (ny - 1)
+        dz = ((e >> 1) + (nz - z)) & (nz - 1)
+        dc = (e + c) & 1
+        return ((dy * row + dz * 2 + dc) * 45) & (n - 1)
+
+    id_row = [turn_of(ids_ref[j : j + 1, :]).astype(F32) for j in range(TOP)]
     id_col = [column(r) for r in id_row]
     gate_col = [column(gates_ref[j : j + 1, :]) for j in range(TOP)]
     place_row, place_col = [], []
@@ -236,7 +230,7 @@
         place_col.append(id_col[j] * CAP + jnp.sum(col_count, axis=1, keepdims=True))
     rows = n * CAP
     r_iota = lax.broadcasted_iota(jnp.int32, (rows, length), 0).astype(F32)
-    spread = jnp.where(
+    spread[...] = jnp.where(
         (r_iota == place_row[0]) | (r_iota == place_row[1]), 1.0, 0.0
     ).astype(BF)
 
@@ -279,62 +273,48 @@
     half = heads // 4
     lax.fori_loop(0, half, inside, 0)
 
-    def mod_y(v):
-        return lax.rem(v + 2 * ny, ny)
-
-    def mod_z(v):
+    def around(v):
         return lax.rem(v + 2 * nz, nz)
 
-    def piece(axis, origin, h, many=1):
-        if axis == 0:
-            return w_all.at[pa, origin, pl.ds(h * (nz // cut), many * (nz // cut))]
-        return w_all.at[pb, pl.ds(h * (ny // cut), many * (ny // cut)), origin]
-
-    def pieces(axis, way, step):
-        size = ny if axis == 0 else nz
+    def piece(origin, h, many=1):
+        return w_all.at[c, origin, pl.ds(h * (nz // cut), many * (nz // cut))]
+
+    def pieces(way, step):
         mine = tuple(range(way * cut // 2, (way + 1) * cut // 2))
-        if 2 * step > size:
+        if 2 * step > nz:
             return ()
-        return mine if 2 * step == size else mine + tuple(set(range(cut)) - set(mine))
+        return mine if 2 * step == nz else mine + tuple(set(range(cut)) - set(mine))
 
     def to_sibling(ref):
         remote(ref, ref, sib_send, sib_recv, sib).start()
 
-    def ring_copy(axis, way, step, h):
-        mod, at = (mod_y, y) if axis == 0 else (mod_z, z)
+    def ring_copy(way, step, h):
         sign = 1 if way == 0 else -1
-        ref = piece(axis, mod(at - sign * (step - 1)), h)
-        dev = seq(mod(at + sign), z, c) if axis == 0 else seq(y, mod(at + sign), c)
-        place = (axis, way, step - 1, h)
+        ref = piece(around(ring_at - sign * (step - 1)), h)
+        to = around(ring_at + sign)
+        dev = seq(to + c * (y - to), z + c * (to - z), c)
+        place = (way, step - 1, h)
         return remote(ref, ref, ring_send.at[place], ring_recv.at[place], dev)
 
     def ring_step(step):
         for turn in range(cut):
-            for axis in (0, 1):
-                mod, at = (mod_y, y) if axis == 0 else (mod_z, z)
-                for way in (0, 1):
-                    order = pieces(axis, way, step)
-                    if turn < len(order):
-                        h = order[turn]
-                        origin = mod(at - step if way == 0 else at + step)
-                        drain(piece(axis, origin, h), ring_recv.at[axis, way, step - 1, h])
-                        if h in pieces(axis, way, step + 1):
-                            ring_copy(axis, way, step + 1, h).start()
-                        if turn == len(order) - 1:
-                            to_sibling(piece(axis, origin, min(order), len(order)))
-
-    def ring_open(axis):
-        for turn in range(cut):
             for way in (0, 1):
-                if turn < len(pieces(axis, way, 1)):
-                    ring_copy(axis, way, 1, pieces(axis, way, 1)[turn]).start()
-
-    drain(w_all.at[pa, y], w1_recv.at[0])
-    ring_open(0)
-    drain(w_all.at[pb, :, z], w1_recv.at[1])
-    ring_open(1)
-    to_sibling(w_all.at[pa, y])
-    to_sibling(w_all.at[pb, :, z])
+                order = pieces(way, step)
+                if turn < len(order):
+                    h = order[turn]
+                    origin = around(ring_at - step if way == 0 else ring_at + step)
+                    drain(piece(origin, h), ring_recv.at[way, step - 1, h])
+                    if h in pieces(way, step + 1):
+                        ring_copy(way, step + 1, h).start()
+                    if turn == len(order) - 1:
+                        to_sibling(piece(origin, min(order), len(order)))
+
+    drain(w_all.at[c, ring_at], w1_recv)
+    for turn in range(cut):
+        for way in (0, 1):
+            if turn < len(pieces(way, 1)):
+                ring_copy(way, 1, pieces(way, 1)[turn]).start()
+    to_sibling(w_all.at[c, ring_at])
 
     lax.fori_loop(half, heads // 2, inside, 0)
 
@@ -404,16 +384,24 @@
     for p in range(hh // 2):
         before(other // 2 + p)
 
-    for step in range(4, max(ny, nz) // 2 + 1):
+    for step in range(4, nz // 2 + 1):
         ring_step(step)
 
-    def project(part):
-        cols = pl.ds(pl.multiple_of(part * quarter, quarter), quarter)
-        return dot(attended[:, cols], w_all[part].reshape(width, quarter), ((1,), (1,)))
-
-    projected = project(pa) + project(pb)
-    drain(w_all.at[pl.ds(2 * (1 - c), 2)], sib_recv)
-    projected = projected + (project(2 * (1 - c)) + project(2 * (1 - c) + 1))
+    def project(h, add):
+        att = attended[:, h * part : (h + 1) * part]
+        rows_of = width // ny
+        for yy in range(ny):
+            w = w_all[0, yy] if h == 0 else w_all[1, :, yy]
+            cols = slice(width + yy * rows_of, width + (yy + 1) * rows_of)
+            got = dot(att, w.reshape(rows_of, part), ((1,), (1,)))
+            intra[:, cols] = intra[:, cols] + got if add else got
+
+    pl.when(c == 0)(functools.partial(project, 0, False))
+    pl.when(c == 1)(functools.partial(project, 1, False))
+    drain(w_all.at[1 - c], sib_recv)
+    pl.when(c == 0)(functools.partial(project, 1, True))
+    pl.when(c == 1)(functools.partial(project, 0, True))
+    projected = intra[:, width : 2 * width]
     hidden = (res_ref[...].astype(F32) + projected).astype(BF)
     hidden_float = hidden.astype(F32)
     intra[:, :width] = hidden_float
@@ -421,7 +409,6 @@
         hidden_float
         * lax.rsqrt(jnp.mean(hidden_float * hidden_float, axis=-1, keepdims=True) + 1e-06)
     ).astype(BF)
-    xb[...] = dot(spread, normed).astype(BF).reshape(n, CAP, width)
 
     def offset(i):
         j = lax.rem(i * 37, n)
@@ -437,14 +424,21 @@
 
     per = n // GROUPS
     pl.semaphore_wait(met, ny - 1)
-    pltpu.make_async_copy(xb.at[me], xr.at[0], x_recv.at[0]).start()
+
+    def fill(g):
+        mine = spread[pl.ds(pl.multiple_of(g * per * CAP, per * CAP), per * CAP)]
+        xb[pl.ds(g * per, per)] = dot(mine, normed).astype(BF).reshape(per, CAP, width)
 
     def dispatch(i, _):
-        to = ahead(i)
-        remote(xb.at[to], xr.at[i], x_send, x_recv.at[i // per], to).start()
-        return 0
-
-    lax.fori_loop(1, n, dispatch, 0)
+        remote(xb.at[i], xr.at[i], x_send, x_recv.at[i // per], ahead(i)).start()
+        return 0
+
+    fill(0)
+    pltpu.make_async_copy(xb.at[0], xr.at[0], x_recv.at[0]).start()
+    lax.fori_loop(1, per, dispatch, 0)
+    for g in range(1, GROUPS):
+        fill(g)
+        lax.fori_loop(g * per, (g + 1) * per, dispatch, 0)
 
     loads[7].wait()
     loads[8].wait()
@@ -460,11 +454,11 @@
 
     def give_back(i, _):
         to = behind(i)
-        remote(yb.at[i], ret.at[me], y_send, y_recv, to).start()
+        remote(yb.at[i], ret.at[i], y_send, y_recv.at[i // per], to).start()
         return 0
 
     expert(0)
-    pltpu.make_async_copy(yb.at[0], ret.at[me], y_recv).start()
+    pltpu.make_async_copy(yb.at[0], ret.at[0], y_recv.at[0]).start()
     lax.fori_loop(1, per, give_back, 0)
 
     def group(g, _):
@@ -474,14 +468,20 @@
 
     lax.fori_loop(1, GROUPS, group, 0)
 
-    r_lane = lax.broadcasted_iota(jnp.int32, (length, rows), 1).astype(F32)
-    picks = jnp.concatenate(
-        [jnp.where(r_lane == place_col[j], 1.0, 0.0).astype(BF) for j in range(TOP)], axis=0
-    )
-    drain(ret, y_recv)
-    back = ret[...].reshape(rows, width)
-    picked = dot(picks, back)
-    combined = picked[:length] * gate_col[0] + picked[length:] * gate_col[1]
+    wide = per * CAP
+    r_lane = lax.broadcasted_iota(jnp.int32, (length, wide), 1).astype(F32)
+    combined = jnp.zeros((length, width), F32)
+    for g in range(GROUPS):
+        picks = jnp.concatenate(
+            [
+                jnp.where(r_lane + g * wide == place_col[j], 1.0, 0.0).astype(BF)
+                for j in range(TOP)
+            ],
+            axis=0,
+        )
+        drain(ret.at[pl.ds(g * per, per)], y_recv.at[g])
+        picked = dot(picks, ret[g * per : (g + 1) * per].reshape(wide, width))
+        combined = combined + (picked[:length] * gate_col[0] + picked[length:] * gate_col[1])
     o_ref[...] = (intra[:, :width] + combined).astype(BF)
 
     drain(s_sib, s0_send)
@@ -489,16 +489,13 @@
     drain(r2.at[pl.ds(0, ny - 1)], s2_send)
     drain(r3.at[pl.ds(0, nz - 1)], s3_send)
     drain(s_sib, s4_send)
-    drain(w_all.at[0, 0, pl.ds(0, nz - 1)], w1_send.at[0])
-    drain(w_loc.at[0], w1_send.at[0])
-    drain(w_all.at[0, pl.ds(0, ny - 1), 0], w1_send.at[1])
-    drain(w_loc.at[0], w1_send.at[1])
-    for axis in (0, 1):
-        for step in range(1, max(ny, nz) // 2 + 1):
-            for way in (0, 1):
-                for h in pieces(axis, way, step):
-                    ring_copy(axis, way, step, h).wait_send()
-    drain(w_all.at[pl.ds(2 * c, 2)], sib_send)
+    drain(w_all.at[0, 0, pl.ds(0, nz - 1)], w1_send)
+    drain(w_loc.at[0], w1_send)
+    for step in range(1, nz // 2 + 1):
+        for way in (0, 1):
+            for h in pieces(way, step):
+                ring_copy(way, step, h).wait_send()
+    drain(w_all.at[c], sib_send)
     drain(xb.at[pl.ds(0, n - 1)], x_send)
     drain(yb.at[pl.ds(0, n - 1)], y_send)
 
@@ -507,7 +504,8 @@
     n = ny * nz * 2
     length, width = res.shape
     cols = wt.shape[0]
-    quarter = heads * dv // 4
+    part = heads * dv // 2
+    assert ny == nz
     vmem = pl.BlockSpec(memory_space=pltpu.VMEM)
     hbm = pl.BlockSpec(memory_space=pl.ANY)
     steps = max(ny, nz) // 2
@@ -530,28 +528,27 @@
             pltpu.VMEM((ny, dk, dv), BF),
             pltpu.VMEM((nz, dk, dv), BF),
             pltpu.VMEM((heads, dk, dv), BF),
-            pltpu.VMEM((4, cols, quarter), BF),
-            pltpu.VMEM((4, ny, nz, 2, cols, quarter), BF),
+            pltpu.VMEM((2, cols, part), BF),
+            pltpu.VMEM((2, ny, nz, 2, cols, part), BF),
             pltpu.VMEM((length, heads * dv), F32),
             pltpu.VMEM((length, heads * dv), BF),
             pltpu.VMEM(w_in.shape, BF),
             pltpu.VMEM(w_out.shape, BF),
+            pltpu.VMEM((n * CAP, length), BF),
             pltpu.VMEM(rows, BF),
             pltpu.VMEM(rows, BF),
             pltpu.VMEM(rows, BF),
             pltpu.VMEM(rows, BF),
-            *[dma] * 10,
-            dma((2,)),
-            dma((2,)),
+            *[dma] * 12,
             pltpu.SemaphoreType.REGULAR,
-            dma((2, 2, steps, 4)),
-            dma((2, 2, steps, 4)),
+            dma((2, steps, 4)),
+            dma((2, steps, 4)),
             dma,
             dma,
             dma,
             dma((GROUPS,)),
             dma,
-            dma,
+            dma((GROUPS,)),
             dma((9,)),
         ],
         compiler_params=pltpu.CompilerParams(

time: 97.1 us -> 97.5 us (level)
  no operation moved by 1% of the time
where the time goes in v4:
time: 97.5 us; the launch traced here: 97.3 us
  Pallas kernels  95.7 us (98%)
  local copies, waits for them, and re-layouts  1.67 us (2%)
    pallas_call x1, Pallas kernels, layer(): pl.pallas_call(functools.partial(layer_kernel, ny, nz, heads, dk, dv), ou...  95.7 us

profile of v4, /device:TPU:1, one launch (start us, length us, event | category | flops | bytes accessed | tf_op | source)
XLA Modules:
  0.0 97.3 jit_solution(8012687495986601406)
XLA Ops:
  0.0 95.7 %layer.1 = bf16[128,1024]{1,0:T(8,128)(2,1)} custom-call(bf16[128,1024]{1,0:T(8,128)(2,1)} %q_hbm.1, bf16[128,1024]{1,0:T(8,128)(2,1)} %k_hbm.1, bf16[128,2048]{1,0:T(8,128)(2,1)} %v_hbm.1, bf16[128,1024]{1,0:T(8,128)(2,1)} %res_hbm.1, bf16[8,2048]{1,0:T(8,128)(2,1)} %bitcast.7, bf16[1024,768]{1,0:T(8,128)(2,1)} %bitcast.5, bf16[384,1024]{1,0:T(8,128)(2,1)} %bitcast.6, ...), custom_call_target="tpu_custom_call" | custom-call | tf_op jit(solution)/shard_map/layer/pallas_call | solution.py:514
  95.7 1.7 %copy.11 = bf16[128,1024]{1,0:T(8,128)(2,1)} copy(bf16[128,1024]{1,0:T(8,128)(2,1)} %layer.1) | data formatting | bytes 524288

commit v5 on v3

--- a/solution.py
+++ b/solution.py
@@ -58,6 +58,7 @@
     attended,
     win,
     wout,
+    spread,
     xb,
     xr,
     yb,
@@ -223,7 +224,13 @@
     def column(r):
         return jnp.sum(jnp.where(eye, r, 0.0), axis=1, keepdims=True)
 
-    id_row = [ids_ref[j : j + 1, :].astype(F32) for j in range(TOP)]
+    def turn_of(e):
+        dy = ((e >> (row.bit_length() - 1)) + (ny - y)) & (ny - 1)
+        dz = ((e >> 1) + (nz - z)) & (nz - 1)
+        dc = (e + c) & 1
+        return ((dy * row + dz * 2 + dc) * 45) & (n - 1)
+
+    id_row = [turn_of(ids_ref[j : j + 1, :]).astype(F32) for j in range(TOP)]
     id_col = [column(r) for r in id_row]
     gate_col = [column(gates_ref[j : j + 1, :]) for j in range(TOP)]
     place_row, place_col = [], []
@@ -236,7 +243,7 @@
         place_col.append(id_col[j] * CAP + jnp.sum(col_count, axis=1, keepdims=True))
     rows = n * CAP
     r_iota = lax.broadcasted_iota(jnp.int32, (rows, length), 0).astype(F32)
-    spread = jnp.where(
+    spread[...] = jnp.where(
         (r_iota == place_row[0]) | (r_iota == place_row[1]), 1.0, 0.0
     ).astype(BF)
 
@@ -246,8 +253,11 @@
         s_pair[i] = both.astype(BF)
     pltpu.make_async_copy(s_pair.at[z], r1.at[z], s1_recv).start()
 
+    def far_first(i, size):
+        return size // 2 + (1 - 2 * lax.rem(i, 2)) * (i // 2) + size
+
     def phase1(i, _):
-        to = lax.rem(z + i, nz)
+        to = lax.rem(z + far_first(i, nz), nz)
         remote(s_pair.at[to], r1.at[z], s1_send, s1_recv, seq(y, to, c)).start()
         return 0
 
@@ -346,7 +356,7 @@
     pltpu.make_async_copy(tot, r2.at[y], s2_recv).start()
 
     def phase2(i, _):
-        yy = lax.rem(y + i, ny)
+        yy = lax.rem(y + far_first(i, ny), ny)
         remote(tot, r2.at[y], s2_send, s2_recv, seq(yy, z, c)).start()
         return 0
 
@@ -365,7 +375,7 @@
     pltpu.make_async_copy(p_out.at[z], r3.at[z], s3_recv).start()
 
     def phase3(i, _):
-        to = lax.rem(z + i, nz)
+        to = lax.rem(z + far_first(i, nz), nz)
         remote(p_out.at[to], r3.at[z], s3_send, s3_recv, seq(y, to, c)).start()
         return 0
 
@@ -421,7 +431,6 @@
         hidden_float
         * lax.rsqrt(jnp.mean(hidden_float * hidden_float, axis=-1, keepdims=True) + 1e-06)
     ).astype(BF)
-    xb[...] = dot(spread, normed).astype(BF).reshape(n, CAP, width)
 
     def offset(i):
         j = lax.rem(i * 37, n)
@@ -437,14 +446,21 @@
 
     per = n // GROUPS
     pl.semaphore_wait(met, ny - 1)
-    pltpu.make_async_copy(xb.at[me], xr.at[0], x_recv.at[0]).start()
+
+    def fill(g):
+        mine = spread[pl.ds(pl.multiple_of(g * per * CAP, per * CAP), per * CAP)]
+        xb[pl.ds(g * per, per)] = dot(mine, normed).astype(BF).reshape(per, CAP, width)
 
     def dispatch(i, _):
-        to = ahead(i)
-        remote(xb.at[to], xr.at[i], x_send, x_recv.at[i // per], to).start()
-        return 0
-
-    lax.fori_loop(1, n, dispatch, 0)
+        remote(xb.at[i], xr.at[i], x_send, x_recv.at[i // per], ahead(i)).start()
+        return 0
+
+    fill(0)
+    pltpu.make_async_copy(xb.at[0], xr.at[0], x_recv.at[0]).start()
+    lax.fori_loop(1, per, dispatch, 0)
+    for g in range(1, GROUPS):
+        fill(g)
+        lax.fori_loop(g * per, (g + 1) * per, dispatch, 0)
 
     loads[7].wait()
     loads[8].wait()
@@ -460,11 +476,11 @@
 
     def give_back(i, _):
         to = behind(i)
-        remote(yb.at[i], ret.at[me], y_send, y_recv, to).start()
+        remote(yb.at[i], ret.at[i], y_send, y_recv.at[i // per], to).start()
         return 0
 
     expert(0)
-    pltpu.make_async_copy(yb.at[0], ret.at[me], y_recv).start()
+    pltpu.make_async_copy(yb.at[0], ret.at[0], y_recv.at[0]).start()
     lax.fori_loop(1, per, give_back, 0)
 
     def group(g, _):
@@ -474,14 +490,20 @@
 
     lax.fori_loop(1, GROUPS, group, 0)
 
-    r_lane = lax.broadcasted_iota(jnp.int32, (length, rows), 1).astype(F32)
-    picks = jnp.concatenate(
-        [jnp.where(r_lane == place_col[j], 1.0, 0.0).astype(BF) for j in range(TOP)], axis=0
-    )
-    drain(ret, y_recv)
-    back = ret[...].reshape(rows, width)
-    picked = dot(picks, back)
-    combined = picked[:length] * gate_col[0] + picked[length:] * gate_col[1]
+    wide = per * CAP
+    r_lane = lax.broadcasted_iota(jnp.int32, (length, wide), 1).astype(F32)
+    combined = jnp.zeros((length, width), F32)
+    for g in range(GROUPS):
+        picks = jnp.concatenate(
+            [
+                jnp.where(r_lane + g * wide == place_col[j], 1.0, 0.0).astype(BF)
+                for j in range(TOP)
+            ],
+            axis=0,
+        )
+        drain(ret.at[pl.ds(g * per, per)], y_recv.at[g])
+        picked = dot(picks, ret[g * per : (g + 1) * per].reshape(wide, width))
+        combined = combined + (picked[:length] * gate_col[0] + picked[length:] * gate_col[1])
     o_ref[...] = (intra[:, :width] + combined).astype(BF)
 
     drain(s_sib, s0_send)
@@ -515,7 +537,7 @@
     rows = (n, CAP, width)
     return pl.pallas_call(
         functools.partial(layer_kernel, ny, nz, heads, dk, dv),
-        out_shape=jax.ShapeDtypeStruct((length, width), BF),
+        out_shape=pltpu.VMEM((length, width), BF),
         in_specs=[hbm] * 9,
         out_specs=vmem,
         scratch_shapes=[
@@ -536,6 +558,7 @@
             pltpu.VMEM((length, heads * dv), BF),
             pltpu.VMEM(w_in.shape, BF),
             pltpu.VMEM(w_out.shape, BF),
+            pltpu.VMEM((n * CAP, length), BF),
             pltpu.VMEM(rows, BF),
             pltpu.VMEM(rows, BF),
             pltpu.VMEM(rows, BF),
@@ -551,7 +574,7 @@
             dma,
             dma((GROUPS,)),
             dma,
-            dma,
+            dma((GROUPS,)),
             dma((9,)),
         ],
         compiler_params=pltpu.CompilerParams(

time: 97.1 us -> 94.8 us (0.976)
  Pallas kernels: 95.2 us -> 94 us
    pallas_call x1, Pallas kernels: 95.2 us -> 94 us  [layer(): pl.pallas_call(functools.partial(layer_kernel, ny, nz, heads, dk, dv), ou...]
where the time goes in v5:
time: 94.8 us; the launch traced here: 94.7 us
  Pallas kernels  94 us (99%)
    pallas_call x1, Pallas kernels, layer(): pl.pallas_call(functools.partial(layer_kernel, ny, nz, heads, dk, dv), ou...  94 us

profile of v5, /device:TPU:1, one launch (start us, length us, event | category | flops | bytes accessed | tf_op | source)
XLA Modules:
  0.0 94.7 jit_solution(4110205229515672223)
XLA Ops:
  0.0 94.0 %layer.1 = bf16[128,1024]{1,0:T(8,128)(2,1)S(1)} custom-call(bf16[128,1024]{1,0:T(8,128)(2,1)} %q_hbm.1, bf16[128,1024]{1,0:T(8,128)(2,1)} %k_hbm.1, bf16[128,2048]{1,0:T(8,128)(2,1)} %v_hbm.1, bf16[128,1024]{1,0:T(8,128)(2,1)} %res_hbm.1, bf16[8,2048]{1,0:T(8,128)(2,1)} %bitcast.7, bf16[1024,768]{1,0:T(8,128)(2,1)} %bitcast.5, bf16[384,1024]{1,0:T(8,128)(2,1)} %bitcast.6, ...), custom_call_target="tpu_custom_call" | custom-call | tf_op jit(solution)/shard_map/layer/pallas_call | solution.py:538
  94.0 0.7 copy.11

commit v6 on v5

--- a/solution.py
+++ b/solution.py
@@ -9,7 +9,7 @@
 
 TOP = 2
 CAP = 4
-GROUPS = 4
+GROUPS = 8
 MESH = pl.DeviceIdType.MESH
 BF = jnp.bfloat16
 F32 = jnp.float32

time: 94.8 us -> 94.8 us (level)
  no operation moved by 1% of the time
where the time goes in v6:
time: 94.8 us; the launch traced here: 94.7 us
  Pallas kernels  94 us (99%)
    pallas_call x1, Pallas kernels, layer(): pl.pallas_call(functools.partial(layer_kernel, ny, nz, heads, dk, dv), ou...  94 us

profile of v6, /device:TPU:1, one launch (start us, length us, event | category | flops | bytes accessed | tf_op | source)
XLA Modules:
  0.0 94.7 jit_solution(5230164586347665568)
XLA Ops:
  0.0 94.0 %layer.1 = bf16[128,1024]{1,0:T(8,128)(2,1)S(1)} custom-call(bf16[128,1024]{1,0:T(8,128)(2,1)} %q_hbm.1, bf16[128,1024]{1,0:T(8,128)(2,1)} %k_hbm.1, bf16[128,2048]{1,0:T(8,128)(2,1)} %v_hbm.1, bf16[128,1024]{1,0:T(8,128)(2,1)} %res_hbm.1, bf16[8,2048]{1,0:T(8,128)(2,1)} %bitcast.7, bf16[1024,768]{1,0:T(8,128)(2,1)} %bitcast.5, bf16[384,1024]{1,0:T(8,128)(2,1)} %bitcast.6, ...), custom_call_target="tpu_custom_call" | custom-call | tf_op jit(solution)/shard_map/layer/pallas_call | solution.py:538
  94.0 0.7 copy.11

commit v7 on v5

--- a/solution.py
+++ b/solution.py
@@ -133,15 +133,18 @@
         load.start()
     barrier = pltpu.get_barrier_semaphore()
 
+    def far_first(i, size):
+        return size // 2 + (1 - 2 * lax.rem(i, 2)) * (i // 2) + size
+
     def greet(dev):
         pl.semaphore_signal(barrier, inc=1, device_id={"seq": dev}, device_id_type=MESH)
 
     def greet_row(i, _):
-        greet(y * row + lax.rem(at_row + i, row))
+        greet(y * row + lax.rem(at_row + far_first(i, row), row))
         return 0
 
     def greet_column(i, _):
-        greet(seq(lax.rem(y + i // 2, ny), z, lax.rem(c + i, 2)))
+        greet(seq(lax.rem(y + far_first(i // 2, ny), ny), z, lax.rem(c + i, 2)))
         return 0
 
     sib = seq(y, z, 1 - c)
@@ -159,29 +162,32 @@
         pltpu.make_async_copy(w_loc.at[part], w_all.at[part, y, z, c], sem).start()
 
     def along_z(i, _):
-        to = lax.rem(at_row + i, row)
+        to = lax.rem(at_row + far_first(i, row), row)
         part = 2 * lax.rem(to, 2)
         remote(
             w_loc.at[part], w_all.at[part, y, z, c], w1_send.at[0], w1_recv.at[0], y * row + to
         ).start()
         return 0
 
-    def along_y(i, _):
-        cc = lax.rem(c + i, 2)
+    def to_column(yy, cc):
         part = 2 * cc + 1
         remote(
             w_loc.at[part],
             w_all.at[part, y, z, c],
             w1_send.at[1],
             w1_recv.at[1],
-            seq(lax.rem(y + i // 2, ny), z, cc),
+            seq(yy, z, cc),
         ).start()
+
+    def along_y(i, _):
+        to_column(lax.rem(y + far_first(i // 2, ny), ny), lax.rem(c + i, 2))
         return 0
 
     keep(pa, w1_recv.at[0])
     keep(pb, w1_recv.at[1])
     lax.fori_loop(1, row, along_z, 0)
-    lax.fori_loop(1, 2 * ny, along_y, 0)
+    lax.fori_loop(2, 2 * ny, along_y, 0)
+    to_column(y, 1 - c)
 
     loads[0].wait()
     loads[1].wait()
@@ -252,9 +258,6 @@
         both = s_loc[own + i].astype(F32) + s_sib[i].astype(F32)
         s_pair[i] = both.astype(BF)
     pltpu.make_async_copy(s_pair.at[z], r1.at[z], s1_recv).start()
-
-    def far_first(i, size):
-        return size // 2 + (1 - 2 * lax.rem(i, 2)) * (i // 2) + size
 
     def phase1(i, _):
         to = lax.rem(z + far_first(i, nz), nz)

time: 94.8 us -> 93.4 us (0.985)
  Pallas kernels: 94 us -> 92.6 us
    pallas_call x1, Pallas kernels: 94 us -> 92.6 us  [layer(): pl.pallas_call(functools.partial(layer_kernel, ny, nz, heads, dk, dv), ou...]
where the time goes in v7:
time: 93.4 us; the launch traced here: 93.3 us
  Pallas kernels  92.6 us (99%)
    pallas_call x1, Pallas kernels, layer(): pl.pallas_call(functools.partial(layer_kernel, ny, nz, heads, dk, dv), ou...  92.6 us

profile of v7, /device:TPU:1, one launch (start us, length us, event | category | flops | bytes accessed | tf_op | source)
XLA Modules:
  0.0 93.3 jit_solution(16275152107479718156)
XLA Ops:
  0.0 92.6 %layer.1 = bf16[128,1024]{1,0:T(8,128)(2,1)S(1)} custom-call(bf16[128,1024]{1,0:T(8,128)(2,1)} %q_hbm.1, bf16[128,1024]{1,0:T(8,128)(2,1)} %k_hbm.1, bf16[128,2048]{1,0:T(8,128)(2,1)} %v_hbm.1, bf16[128,1024]{1,0:T(8,128)(2,1)} %res_hbm.1, bf16[8,2048]{1,0:T(8,128)(2,1)} %bitcast.7, bf16[1024,768]{1,0:T(8,128)(2,1)} %bitcast.5, bf16[384,1024]{1,0:T(8,128)(2,1)} %bitcast.6, ...), custom_call_target="tpu_custom_call" | custom-call | tf_op jit(solution)/shard_map/layer/pallas_call | solution.py:541
  92.6 0.7 copy.11

commit v8 on v7

--- a/solution.py
+++ b/solution.py
@@ -192,16 +192,21 @@
     loads[0].wait()
     loads[1].wait()
 
-    for p in range(heads // 2):
-        kp = k_ref[:, 2 * p * dk : 2 * (p + 1) * dk]
-        kv = dot(kp, v_ref[:, 2 * p * dv : 2 * (p + 1) * dv], ((0,), (0,)))
+    def state(p):
+        kp = k_ref[:, pl.ds(pl.multiple_of(p * 2 * dk, 2 * dk), 2 * dk)]
+        vp = v_ref[:, pl.ds(pl.multiple_of(p * 2 * dv, 2 * dv), 2 * dv)]
+        kv = dot(kp, vp, ((0,), (0,)))
         s_loc[2 * p] = kv[:dk, :dv].astype(BF)
         s_loc[2 * p + 1] = kv[dk:, dv:].astype(BF)
 
     hh = heads // 2
     own, other = c * hh, (1 - c) * hh
     first_core = c == 0
+    for p in range(hh // 2):
+        state(other // 2 + p)
     remote(s_loc.at[pl.ds(other, hh)], s_sib, s0_send, s0_recv, sib).start()
+    for p in range(hh // 2):
+        state(own // 2 + p)
 
     def tell(cc, yy):
         pl.semaphore_signal(

time: 93.4 us -> 93.2 us (level)
  no operation moved by 1% of the time
where the time goes in v8:
time: 93.2 us; the launch traced here: 93.1 us
  Pallas kernels  92.4 us (99%)
    pallas_call x1, Pallas kernels, layer(): pl.pallas_call(functools.partial(layer_kernel, ny, nz, heads, dk, dv), ou...  92.4 us

profile of v8, /device:TPU:1, one launch (start us, length us, event | category | flops | bytes accessed | tf_op | source)
XLA Modules:
  0.0 93.1 jit_solution(17076371685795618852)
XLA Ops:
  0.0 92.4 %layer.1 = bf16[128,1024]{1,0:T(8,128)(2,1)S(1)} custom-call(bf16[128,1024]{1,0:T(8,128)(2,1)} %q_hbm.1, bf16[128,1024]{1,0:T(8,128)(2,1)} %k_hbm.1, bf16[128,2048]{1,0:T(8,128)(2,1)} %v_hbm.1, bf16[128,1024]{1,0:T(8,128)(2,1)} %res_hbm.1, bf16[8,2048]{1,0:T(8,128)(2,1)} %bitcast.7, bf16[1024,768]{1,0:T(8,128)(2,1)} %bitcast.5, bf16[384,1024]{1,0:T(8,128)(2,1)} %bitcast.6, ...), custom_call_target="tpu_custom_call" | custom-call | tf_op jit(solution)/shard_map/layer/pallas_call | solution.py:546
  92.4 0.7 copy.11
